TPU v7x, 32 devices: a whole 2x2x4 slice. The times are simulated.
32 devices in a mesh: img: 8 (over z, y), row: 4 (over x, core).
Axes of the slice: x: 2, y: 2, z: 4, core: 2. Of those that a mesh axis runs over, the one named last changes fastest.
Arguments:
- stem_input: bfloat16 [32, 96, 96, 64], P('img', 'row'), may hold values from -6 to 6
- group: int32 [32], P('img'), may hold values 0 or 1
- conv_in: bfloat16 [64, 64], replicated, may hold values from -0.75 to 0.75
- conv_mid: bfloat16 [64, 9, 64], replicated, may hold values from -0.25 to 0.25
- conv_out: bfloat16 [64, 256], replicated, may hold values from -0.75 to 0.75
- conv_skip: bfloat16 [64, 256], replicated, may hold values from -0.75 to 0.75
- norm_gain: float32 [384], replicated, may hold values from 0.5 to 1.5
- norm_bias: float32 [384], replicated, may hold values from -4 to 4
- patch_weight: bfloat16 [4096, 768], replicated, may hold values from -0.09375 to 0.09375
- patch_bias: float32 [768], replicated, may hold values from -6 to 6
- attn_gain: float32 [768], replicated, may hold values from 0.5 to 1.5
- attn_bias: float32 [768], replicated, may hold values from -4 to 4
- qkv_weight: bfloat16 [768, 2304], replicated, may hold values from -0.21875 to 0.21875
- out_weight: bfloat16 [768, 768], replicated, may hold values from -1.75 to 1.75
- mlp_gain: float32 [768], replicated, may hold values from 0.5 to 1.5
- mlp_bias: float32 [768], replicated, may hold values from -4 to 4
- up_weight: bfloat16 [768, 3072], replicated, may hold values from -0.21875 to 0.21875
- up_bias: float32 [3072], replicated, may hold values from -6 to 6
- down_weight: bfloat16 [3072, 768], replicated, may hold values from -0.109375 to 0.109375
- down_bias: float32 [768], replicated, may hold values from -4 to 4
- cotangent: bfloat16 [32, 576, 768], P('img', 'row'), may hold values from -6 to 6
Outputs:
- block_out: bfloat16 [32, 576, 768], P('img', 'row')
- input_grad: float32 [32, 96, 96, 64], P('img', 'row')
- grad_conv_in: float32 [64, 64], P('row')
- grad_conv_mid: float32 [64, 9, 64], P('row')
- grad_conv_out: float32 [64, 256], P('row')
- grad_conv_skip: float32 [64, 256], P('row')
- grad_norm_gain: float32 [384], P('row')
- grad_norm_bias: float32 [384], P('row')
- grad_patch_weight: float32 [4096, 768], P('row')
- grad_patch_bias: float32 [768], P('row')
- grad_attn_gain: float32 [768], P('row')
- grad_attn_bias: float32 [768], P('row')
- grad_qkv_weight: float32 [768, 2304], P('row')
- grad_out_weight: float32 [768, 768], P('row')
- grad_mlp_gain: float32 [768], P('row')
- grad_mlp_bias: float32 [768], P('row')
- grad_up_weight: float32 [768, 3072], P('row')
- grad_up_bias: float32 [3072], P('row')
- grad_down_weight: float32 [3072, 768], P('row')
- grad_down_bias: float32 [768], P('row')
Inputs may be any that keep to these rules, and one draw needn't show every extreme that they name: `group`: 0 marks a 224px image, whose valid cells are the top left 56 x 56 of its map; 1 a 384px image, all 96 x 96 cells valid.
All inputs are finite; a program needn't handle non-finite values. No bound on the sum of `group` on one device may be relied on, other than what follows from the above.
Results may differ from a plain program's by a relative error of at most 0.017.
Values may be sent and summed in bfloat16 or wider, within the bound.
No kernel may reach another device: no remote copies, remote signals or barrier semaphores. Data moves between devices by JAX's collectives and lax.ppermute only.
A program may use at most 256 MiB of HBM per device.

v0:
```python
import jax
import jax.numpy as jnp
from jax import lax
from jax.sharding import PartitionSpec as P

GROUPS = 32
HEADS = 12
HEAD_DIM = 64
PATCH = 4
FULL = 96
SMALL = 56


def padded_2(cells, sides, width):
    for axis, dim in sides:
        count = lax.axis_size(axis)
        ends = count - 1
        head = lax.slice_in_dim(cells, 0, width, axis=dim)
        tail = lax.slice_in_dim(cells, cells.shape[dim] - width, cells.shape[dim], axis=dim)
        cells = jnp.concatenate(
            [
                lax.ppermute(tail, axis, [(i, (i + 1) % count) for i in range(ends)]),
                cells,
                lax.ppermute(head, axis, [((i + 1) % count, i) for i in range(ends)]),
            ],
            axis=dim,
        )
    return cells


def smooth_gelu(values):
    return jax.nn.gelu(values, approximate=False)


def layer_norm(values, gain, bias):
    mean = jnp.mean(values, axis=-1, keepdims=True)
    centered = values - mean
    return (
        centered * lax.rsqrt(jnp.mean(centered * centered, axis=-1, keepdims=True) + 1e-05) * gain
        + bias
    )


def norm_forward(values, mask_chan, cells, gain, bias):
    images, row_count, col_count, chans = values.shape
    per_group = chans // GROUPS
    split = (images, row_count * col_count, GROUPS, per_group)
    masked = values * mask_chan
    first_sum = jnp.sum(masked.reshape(split), axis=(1, 3))
    second_sum = jnp.sum((masked * values).reshape(split), axis=(1, 3))
    first_sum, second_sum = lax.psum((first_sum, second_sum), "row")
    count = (cells * per_group)[:, None]
    mean = first_sum / count
    rstd = lax.rsqrt(second_sum / count - mean * mean + 1e-05)
    normal = ((values.reshape(split) - mean[:, None, :, None]) * rstd[:, None, :, None]).reshape(
        values.shape
    )
    return (normal * gain + bias, normal, rstd)


def norm_backward(gradient, normal, rstd, mask_chan, cells, gain):
    images, row_count, col_count, chans = gradient.shape
    per_group = chans // GROUPS
    split = (images, row_count * col_count, GROUPS, per_group)
    scaled = gradient * gain
    first_sum = jnp.sum(scaled.reshape(split), axis=(1, 3))
    second_sum = jnp.sum((scaled * normal).reshape(split), axis=(1, 3))
    first_sum, second_sum = lax.psum((first_sum, second_sum), "row")
    count = (cells * per_group)[:, None]
    inner = (
        scaled.reshape(split)
        - (first_sum / count)[:, None, :, None]
        - normal.reshape(split) * (second_sum / count)[:, None, :, None]
    )
    result = (inner * rstd[:, None, :, None]).reshape(gradient.shape) * mask_chan
    return (result, jnp.sum(gradient * normal, axis=(0, 1, 2)), jnp.sum(gradient, axis=(0, 1, 2)))


def tap_stack(padded, row_count, col_count, flipped):
    pieces = []
    for offset in range(9):
        shift_row = offset // 3
        shift_col = offset % 3
        if flipped:
            shift_row = 2 - shift_row
            shift_col = 2 - shift_col
        pieces.append(
            padded[:, shift_row : shift_row + row_count, shift_col : shift_col + col_count]
        )
    return jnp.stack(pieces, axis=3)


def gelu_grad(point, gradient):
    unused, pull = jax.vjp(smooth_gelu, point)
    return pull(gradient)[0]


def per_device(
    stem_input,
    group,
    conv_in,
    conv_mid,
    conv_out,
    conv_skip,
    norm_gain,
    norm_bias,
    patch_weight,
    patch_bias,
    attn_gain,
    attn_bias,
    qkv_weight,
    out_weight,
    mlp_gain,
    mlp_bias,
    up_weight,
    up_bias,
    down_weight,
    down_bias,
    cotangent,
):
    f32 = jnp.float32
    bf16 = jnp.bfloat16
    images, row_count, col_count, chans = stem_input.shape
    wide = conv_out.shape[1]
    width = patch_weight.shape[1]
    row_axis = lax.axis_size("row")
    row_start = lax.axis_index("row") * row_count
    image_side = jnp.where(group == 1, FULL, SMALL).astype(jnp.int32)
    row_inside = (row_start + jnp.arange(row_count))[None, :] < image_side[:, None]
    col_inside = jnp.arange(col_count)[None, :] < image_side[:, None]
    cell_mask = (row_inside[:, :, None] & col_inside[:, None, :]).astype(f32)
    mask_chan = cell_mask[..., None]
    cells = (image_side * image_side).astype(f32)
    inputs = stem_input * mask_chan.astype(bf16)
    first_conv = jnp.einsum("irwc,cd->irwd", inputs, conv_in, preferred_element_type=f32)
    first_norm, first_normal, first_rstd = norm_forward(
        first_conv, mask_chan, cells, norm_gain[:chans], norm_bias[:chans]
    )
    first_act = (smooth_gelu(first_norm) * mask_chan).astype(bf16)
    edged = padded_2(first_act, (("row", 1),), 1)
    padded = jnp.pad(edged, ((0, 0), (0, 0), (1, 1), (0, 0)))
    forward_taps = tap_stack(padded, row_count, col_count, False)
    mid_conv = jnp.einsum("irwtc,ctd->irwd", forward_taps, conv_mid, preferred_element_type=f32)
    mid_norm, mid_normal, mid_rstd = norm_forward(
        mid_conv, mask_chan, cells, norm_gain[chans : 2 * chans], norm_bias[chans : 2 * chans]
    )
    mid_act = (smooth_gelu(mid_norm) * mask_chan).astype(bf16)
    last_conv = jnp.einsum("irwc,cd->irwd", mid_act, conv_out, preferred_element_type=f32)
    skip_conv = jnp.einsum("irwc,cd->irwd", inputs, conv_skip, preferred_element_type=f32)
    last_norm, last_normal, last_rstd = norm_forward(
        last_conv, mask_chan, cells, norm_gain[2 * chans :], norm_bias[2 * chans :]
    )
    joined = last_norm + skip_conv
    stem = (smooth_gelu(joined) * mask_chan).astype(bf16)
    tok_rows = row_count // PATCH
    tok_cols = col_count // PATCH
    local_tok = tok_rows * tok_cols
    all_tok = local_tok * row_axis
    patches = (
        stem.reshape(images, tok_rows, PATCH, tok_cols, PATCH, wide)
        .transpose(0, 1, 3, 2, 4, 5)
        .reshape(images, local_tok, PATCH * PATCH * wide)
    )
    hidden = (
        jnp.einsum("itp,pd->itd", patches, patch_weight, preferred_element_type=f32) + patch_bias
    )
    limit = (image_side // PATCH)[:, None]
    local_pos = jnp.arange(local_tok)
    token_keep = (
        ((lax.axis_index("row") * tok_rows + local_pos // tok_cols)[None, :] < limit)
        & ((local_pos % tok_cols)[None, :] < limit)
    ).astype(f32)
    key_pos = jnp.arange(all_tok)
    key_keep = ((key_pos // tok_cols)[None, :] < limit) & ((key_pos % tok_cols)[None, :] < limit)
    normed = layer_norm(hidden, attn_gain, attn_bias).astype(bf16)
    qkv_local = jnp.einsum("itd,de->ite", normed, qkv_weight, preferred_element_type=f32).astype(
        bf16
    )
    qkv_local = qkv_local.reshape(images, local_tok, 3, HEADS, HEAD_DIM)
    spread = lax.all_to_all(qkv_local, "row", split_axis=3, concat_axis=1, tiled=True)
    query = spread[:, :, 0]
    key_part = spread[:, :, 1]
    value_part = spread[:, :, 2]
    score_scale = HEAD_DIM ** (-0.5)

    def attend_probs(query, key_part):
        scores = (
            jnp.einsum("iqhe,ikhe->ihqk", query, key_part, preferred_element_type=f32) * score_scale
        )
        scores = jnp.where(key_keep[:, None, None, :], scores, -1000000000.0)
        row_top = jnp.max(scores, axis=3, keepdims=True)
        expo = jnp.exp(scores - row_top)
        return expo / jnp.sum(expo, axis=3, keepdims=True)

    probs = attend_probs(query, key_part)
    mixed = jnp.einsum(
        "ihqk,ikhe->iqhe", probs.astype(bf16), value_part, preferred_element_type=f32
    ).astype(bf16)
    back_tokens = lax.all_to_all(mixed, "row", split_axis=1, concat_axis=2, tiled=True)
    attended = back_tokens.reshape(images, local_tok, width)
    hidden2 = hidden + jnp.einsum("ite,ed->itd", attended, out_weight, preferred_element_type=f32)
    normed2 = layer_norm(hidden2, mlp_gain, mlp_bias).astype(bf16)
    pre_act = jnp.einsum("itd,df->itf", normed2, up_weight, preferred_element_type=f32) + up_bias
    activ = smooth_gelu(pre_act).astype(bf16)
    final = (
        hidden2
        + jnp.einsum("itf,fd->itd", activ, down_weight, preferred_element_type=f32)
        + down_bias
    )
    block_out = (final * token_keep[..., None]).astype(bf16)
    grad_final = cotangent.astype(f32) * token_keep[..., None]
    grad_down_bias = jnp.sum(grad_final, axis=(0, 1))
    grad_final_low = grad_final.astype(bf16)
    grad_down_weight = jnp.einsum("itf,itd->fd", activ, grad_final_low, preferred_element_type=f32)
    grad_activ = jnp.einsum("itd,fd->itf", grad_final_low, down_weight, preferred_element_type=f32)
    grad_pre = gelu_grad(pre_act, grad_activ)
    grad_up_bias = jnp.sum(grad_pre, axis=(0, 1))
    grad_pre_low = grad_pre.astype(bf16)
    grad_up_weight = jnp.einsum("itd,itf->df", normed2, grad_pre_low, preferred_element_type=f32)
    grad_normed2 = jnp.einsum("itf,df->itd", grad_pre_low, up_weight, preferred_element_type=f32)
    unused, mlp_pull = jax.vjp(layer_norm, hidden2, mlp_gain, mlp_bias)
    grad_hidden2_ln, grad_mlp_gain, grad_mlp_bias = mlp_pull(grad_normed2)
    grad_hidden2 = grad_final + grad_hidden2_ln
    grad_hidden2_low = grad_hidden2.astype(bf16)
    grad_out_weight = jnp.einsum(
        "ite,itd->ed", attended, grad_hidden2_low, preferred_element_type=f32
    )
    grad_attended = jnp.einsum(
        "itd,ed->ite", grad_hidden2_low, out_weight, preferred_element_type=f32
    ).astype(bf16)
    grad_attended = grad_attended.reshape(images, local_tok, HEADS, HEAD_DIM)
    grad_mixed = lax.all_to_all(grad_attended, "row", split_axis=2, concat_axis=1, tiled=True)
    probs_again = attend_probs(query, key_part)
    grad_value = jnp.einsum(
        "ihqk,iqhe->ikhe", probs_again.astype(bf16), grad_mixed, preferred_element_type=f32
    )
    grad_probs = jnp.einsum("iqhe,ikhe->ihqk", grad_mixed, value_part, preferred_element_type=f32)
    grad_scores = probs_again * (
        grad_probs - jnp.sum(grad_probs * probs_again, axis=3, keepdims=True)
    )
    grad_scores = grad_scores.astype(bf16)
    grad_query = (
        jnp.einsum("ihqk,ikhe->iqhe", grad_scores, key_part, preferred_element_type=f32)
        * score_scale
    )
    grad_key = (
        jnp.einsum("ihqk,iqhe->ikhe", grad_scores, query, preferred_element_type=f32) * score_scale
    )
    stacked = jnp.stack([grad_query, grad_key, grad_value], axis=2).astype(bf16)
    grad_qkv = lax.all_to_all(stacked, "row", split_axis=1, concat_axis=3, tiled=True)
    grad_qkv = grad_qkv.reshape(images, local_tok, 3 * width)
    grad_qkv_weight = jnp.einsum("itd,ite->de", normed, grad_qkv, preferred_element_type=f32)
    grad_normed = jnp.einsum("ite,de->itd", grad_qkv, qkv_weight, preferred_element_type=f32)
    unused, attn_pull = jax.vjp(layer_norm, hidden, attn_gain, attn_bias)
    grad_hidden_ln, grad_attn_gain, grad_attn_bias = attn_pull(grad_normed)
    grad_hidden = grad_hidden2 + grad_hidden_ln
    grad_patch_bias = jnp.sum(grad_hidden, axis=(0, 1))
    grad_hidden_low = grad_hidden.astype(bf16)
    grad_patch_weight = jnp.einsum(
        "itp,itd->pd", patches, grad_hidden_low, preferred_element_type=f32
    )
    grad_patches = jnp.einsum(
        "itd,pd->itp", grad_hidden_low, patch_weight, preferred_element_type=f32
    )
    grad_stem = (
        grad_patches.reshape(images, tok_rows, tok_cols, PATCH, PATCH, wide)
        .transpose(0, 1, 3, 2, 4, 5)
        .reshape(images, row_count, col_count, wide)
    )
    grad_joined = gelu_grad(joined, grad_stem * mask_chan)
    grad_skip_low = grad_joined.astype(bf16)
    grad_conv_skip = jnp.einsum("irwc,irwd->cd", inputs, grad_skip_low, preferred_element_type=f32)
    back_last, last_gain_grad, last_bias_grad = norm_backward(
        grad_joined, last_normal, last_rstd, mask_chan, cells, norm_gain[2 * chans :]
    )
    back_last_low = back_last.astype(bf16)
    grad_conv_out = jnp.einsum("irwc,irwd->cd", mid_act, back_last_low, preferred_element_type=f32)
    grad_mid_act = jnp.einsum("irwd,cd->irwc", back_last_low, conv_out, preferred_element_type=f32)
    grad_mid_norm = gelu_grad(mid_norm, grad_mid_act * mask_chan)
    back_mid, mid_gain_grad, mid_bias_grad = norm_backward(
        grad_mid_norm, mid_normal, mid_rstd, mask_chan, cells, norm_gain[chans : 2 * chans]
    )
    back_mid_low = back_mid.astype(bf16)
    grad_conv_mid = jnp.einsum(
        "irwtc,irwd->ctd", forward_taps, back_mid_low, preferred_element_type=f32
    )
    rimmed = padded_2(back_mid_low, (("row", 1),), 1)
    rim_padded = jnp.pad(rimmed, ((0, 0), (0, 0), (1, 1), (0, 0)))
    back_taps = tap_stack(rim_padded, row_count, col_count, True)
    grad_first_act = jnp.einsum("irwtd,ctd->irwc", back_taps, conv_mid, preferred_element_type=f32)
    grad_first_norm = gelu_grad(first_norm, grad_first_act * mask_chan)
    back_first, first_gain_grad, first_bias_grad = norm_backward(
        grad_first_norm, first_normal, first_rstd, mask_chan, cells, norm_gain[:chans]
    )
    back_first_low = back_first.astype(bf16)
    grad_conv_in = jnp.einsum("irwc,irwd->cd", inputs, back_first_low, preferred_element_type=f32)
    input_grad = (
        jnp.einsum("irwd,cd->irwc", back_first_low, conv_in, preferred_element_type=f32)
        + jnp.einsum("irwd,cd->irwc", grad_skip_low, conv_skip, preferred_element_type=f32)
    ) * mask_chan
    grad_norm_gain = jnp.concatenate([first_gain_grad, mid_gain_grad, last_gain_grad])
    grad_norm_bias = jnp.concatenate([first_bias_grad, mid_bias_grad, last_bias_grad])
    gradients = (
        grad_conv_in,
        grad_conv_mid,
        grad_conv_out,
        grad_conv_skip,
        grad_norm_gain,
        grad_norm_bias,
        grad_patch_weight,
        grad_patch_bias,
        grad_attn_gain,
        grad_attn_bias,
        grad_qkv_weight,
        grad_out_weight,
        grad_mlp_gain,
        grad_mlp_bias,
        grad_up_weight,
        grad_up_bias,
        grad_down_weight,
        grad_down_bias,
    )
    summed = lax.psum(
        (
            gradients[0],
            gradients[1],
            gradients[2],
            gradients[3],
            gradients[4],
            gradients[5],
            gradients[6],
            gradients[7],
            gradients[8],
            gradients[9],
            gradients[10],
            gradients[11],
            gradients[12],
            gradients[13],
            gradients[14],
            gradients[15],
            gradients[16],
            gradients[17],
        ),
        ("img", "row"),
    )
    row_index = lax.axis_index("row")
    shares = tuple(
        (
            lax.dynamic_slice_in_dim(
                entry, row_index * (entry.shape[0] // row_axis), entry.shape[0] // row_axis, 0
            )
            for entry in summed
        )
    )
    return (block_out, input_grad) + tuple(shares)


def solution(mesh):
    in_specs = (
        P("img", "row", None, None),
        P("img"),
        P(),
        P(),
        P(),
        P(),
        P(),
        P(),
        P(),
        P(),
        P(),
        P(),
        P(),
        P(),
        P(),
        P(),
        P(),
        P(),
        P(),
        P(),
        P("img", "row", None),
    )
    out_specs = (
        P("img", "row", None),
        P("img", "row", None, None),
        P("row", None),
        P("row", None, None),
        P("row", None),
        P("row", None),
        P("row"),
        P("row"),
        P("row", None),
        P("row"),
        P("row"),
        P("row"),
        P("row", None),
        P("row", None),
        P("row"),
        P("row"),
        P("row", None),
        P("row"),
        P("row", None),
        P("row"),
    )
    return jax.shard_map(
        per_device, mesh=mesh, in_specs=in_specs, out_specs=out_specs, check_vma=False
    )
```

profile of v0, /device:TPU:0, one launch (start us, length us, event | category | flops | bytes accessed | tf_op | source)
XLA Modules:
  0.0 1804.5 jit_solution(8638340361917295879)
XLA Ops:
  20.2 8.4 all-reduce.9
  36.3 9.8 multiply_convert_fusion.7
  70.2 6.3 all-reduce.8
  82.9 10.0 multiply_convert_fusion.6
  101.2 7.8 all-reduce.7
  113.1 7.9 convert_reduce_fusion
  121.1 23.1 %multiply_convert_fusion.2 = (bf16[4,24,96,256]{3,2,1,0:T(8,128)(2,1)}, f32[4,24,96,256]{3,2,1,0:T(8,128)}) fusion(f32[4,24,96,256]{3,2,1,0:T(8,128)S(1)} %get-tuple-element.221, f32[4,24,96]{2,1,0:T(8,128)S(1)} %copy-done.23, u32[4,96,256]{2,1,0:T(8,128)S(1)} %get-tuple-element.220), kind=kLoop, calls=%fused_computation.23 | loop fusion | flops 160432128 | bytes 24023040 | tf_op jit(solution)/shard_map/convert_element_type | solution.py:154
  144.2 7.8 reshape.402
  152.0 6.5 copy.217
  158.5 8.8 reshape.403
  167.3 7.8 add_reduce_fusion
  180.8 14.5 copy.218
  205.7 53.7 %all-to-all-done = bf16[4,144,3,12,64]{1,4,2,0,3:T(8,128)(2,1)} async-done(((bf16[4,144,3,12,64]{1,4,2,0,3:T(8,128)(2,1)}), bf16[4,144,3,12,64]{1,4,2,0,3:T(8,128)(2,1)}, u32[]{:S(2)}, u32[]{:S(2)}) %all-to-all-start) | async-done | bytes 2654240 | tf_op jit(solution)/shard_map/all_to_all | solution.py:180
  259.5 9.0 copy.221
  268.5 8.7 all_to_all.51
  277.2 11.5 fusion.175
  288.7 8.9 fusion.112
  310.6 12.1 all-to-all-done.1
  334.8 7.5 fusion.75
  342.4 17.1 multiply_convert_fusion.3
  359.5 8.1 fusion.177
  367.6 7.6 multiply_reduce_fusion.13
  394.2 15.9 all-to-all-done.2
  417.8 9.1 fusion.109
  426.9 11.1 multiply_reduce_fusion
  438.1 12.0 multiply_convert_fusion
  456.5 8.2 copy.233
  464.7 7.3 reshape.435
  476.7 10.0 convolution_bitcast_fusion.1
  486.7 6.8 convolution_bitcast_fusion.2
  493.4 14.9 all-to-all-done.3
  508.4 6.7 reshape.436
  515.0 10.2 copy.234
  525.3 7.7 fusion.164
  536.5 9.2 fusion.22
  545.7 8.0 convolution_bitcast_fusion
  553.7 6.6 convolution_bitcast_fusion.3
  560.3 12.3 reshape.408
  572.6 9.8 copy.312
  582.4 12.1 reshape.409
  594.6 18.0 multiply_reduce_fusion.2
  625.5 6.0 multiply_convert_fusion.1
  650.6 10.2 fusion.117
  662.3 7.2 multiply_convert_fusion.10
  673.9 7.4 fusion.60
  694.9 7.2 all-reduce.4
  707.7 44.1 %all-reduce.2 = (f32[64,64]{1,0:T(8,128)S(1)}, f32[384]{0:T(512)S(1)}, f32[384]{0:T(512)S(1)}, f32[768]{0:T(1024)S(1)}, f32[768]{0:T(1024)S(1)}, /*index=5*/f32[...) all-reduce(f32[64,64]{1,0:T(8,128)S(1)} %convolution_bitcast_fusion, ...), channel_id=1, replica_groups=mesh['img'=8,'row'=4] {'img','row'}, use_global_device_ids=true, to_apply=%region_47.48 | all-reduce | flops 12544 | bytes 100352 | tf_op jit(solution)/shard_map/psum | solution.py:323
  761.7 1015.8 %all-reduce.12.cloned.1.call-done = (f32[64,9,64]{0,2,1:T(8,128)}, f32[64,256]{1,0:T(8,128)}, f32[64,256]{1,0:T(8,128)}, f32[4096,768]{1,0:T(8,128)}, f32[768,23...) async-done(((f32[64,9,64]{0,2,1:T(8,128)}, f32[64,256]{1,0:T(8,128)}, f32[64,256]{1,0:T(8,128)}, f32[4096,768]{1,0:T(8,128)}, ...) | async-done | bytes 41173008 | tf_op jit(solution)/shard_map/psum | solution.py:323
  (401 shorter events, 231.9 us)
Async XLA Ops:
  7.2 169.7 %copy-start = (bf16[768,2304]{1,0:T(8,128)(2,1)S(1)}, bf16[768,2304]{1,0:T(8,128)(2,1)}, u32[]{:S(2)}) copy-start(bf16[768,2304]{1,0:T(8,128)(2,1)} %param.33) | copy-start | bytes 10616836
  35.0 11.2 copy-start.64
  36.3 9.9 copy-start.81
  36.3 9.9 copy-start.83
  36.3 14.2 copy-start.92
  36.3 14.8 copy-start.93
  46.2 5.5 collective-permute-start.1
  47.5 4.2 collective-permute-start
  82.9 10.0 copy-start.67
  82.9 10.0 copy-start.22
  82.9 10.0 copy-start.60
  92.9 20.2 %copy-start.77 = (f32[256]{0:T(256)S(1)}, f32[256]{0:T(256)}, u32[]{:S(2)}) copy-start(f32[256]{0:T(256)} %slice.116) | copy-start | bytes 3076
  111.4 9.6 copy-start.56
  121.1 23.1 %copy-start.3 = (f32[4,24,96,256]{3,2,1,0:T(8,128)}, f32[4,24,96,256]{3,2,1,0:T(8,128)S(1)}, u32[]{:S(2)}) copy-start(f32[4,24,96,256]{3,2,1,0:T(8,128)S(1)} %get-tuple-element.221) | copy-start | bytes 28311556
  167.3 9.6 copy-start.100
  200.5 58.9 %all-to-all-start = ((bf16[4,144,3,12,64]{1,4,2,0,3:T(8,128)(2,1)}), bf16[4,144,3,12,64]{1,4,2,0,3:T(8,128)(2,1)}, u32[]{:S(2)}, u32[]{:S(2)}) async-start(bf16[4,144,3,12,64]{1,4,2,0,3:T(8,128)(2,1)} %copy.219), calls=%async_computation | async-start | bytes 9437184 | tf_op jit(solution)/shard_map/all_to_all | solution.py:180
  305.3 17.4 all-to-all-start.1
  334.4 40.8 %copy-start.4 = (f32[4,144,768]{2,1,0:T(8,128)}, f32[4,144,768]{2,1,0:T(8,128)S(1)}, u32[]{:S(2)}) copy-start(f32[4,144,768]{2,1,0:T(8,128)S(1)} %get-tuple-element.227) | copy-start | bytes 5308420
  342.4 17.1 copy-start.30
  342.4 17.1 copy-start.49
  385.4 24.7 %all-to-all-start.2 = ((bf16[4,144,12,64]{1,3,0,2:T(8,128)(2,1)}), bf16[4,144,12,64]{1,3,0,2:T(8,128)(2,1)}, u32[]{:S(2)}, u32[]{:S(2)}) async-start(bf16[4,144,12,64]{1,3,0,2:T(8,128)(2,1)} %copy.227), calls=%async_computation.2 | async-start | bytes 3145728 | tf_op jit(solution)/shard_map/all_to_all | solution.py:232
  472.0 36.3 %all-to-all-start.3 = ((bf16[4,2,165888]{2,1,0:T(2,128)(2,1)}), bf16[4,2,165888]{2,1,0:T(2,128)(2,1)}, u32[]{:S(2)}, u32[]{:S(2)}) async-start(bf16[4,2,165888]{2,1,0:T(2,128)(2,1)} %reshape.435), calls=%async_computation.3 | async-start | bytes 5308416 | tf_op jit(solution)/shard_map/all_to_all | solution.py:250
  476.6 1300.9 %all-reduce.12.cloned.1.call-start = ((), (), s32[]{:S(2)}) async-start(), calls=%async_computation.4 | async-start | bytes 82640896 | tf_op jit(solution)/shard_map/psum | solution.py:323
  476.7 10.0 copy-start.5
  476.7 10.0 copy-start.29
  515.0 10.2 copy-start.43
  515.0 10.2 copy-start.45
  515.0 10.2 copy-start.73
  534.7 10.9 slice-start.2
  536.5 17.2 slice-start
  582.4 12.1 copy-start.24
  582.4 12.1 copy-start.57
  582.4 12.1 copy-start.59
  582.4 12.1 copy-start.78
  594.5 24.1 %copy-start.91 = (f32[4]{0:T(128)S(1)}, f32[4]{0:T(128)}, u32[]{:S(2)}) copy-start(f32[4]{0:T(128)} %get-tuple-element.216) | copy-start | bytes 52
  594.5 24.6 %copy-start.26 = (bf16[4,24,96,64]{2,3,1,0:T(8,128)(2,1)S(1)}, bf16[4,24,96,64]{2,3,1,0:T(8,128)(2,1)}, u32[]{:S(2)}) copy-start(bf16[4,24,96,64]{2,3,1,0:T(8,128)(2,1)} %param.21) | copy-start | bytes 3538948
  594.5 24.6 %copy-start.37 = (bf16[4,24,96]{2,1,0:T(8,128)(2,1)S(1)}, bf16[4,24,96]{2,1,0:T(8,128)(2,1)}, u32[]{:S(2)}) copy-start(bf16[4,24,96]{2,1,0:T(8,128)(2,1)} %copy-done.36) | copy-start | bytes 55300
  634.5 11.7 copy-start.79
  662.3 11.6 copy-start.62
  669.5 11.7 collective-permute-start.3
  670.8 10.4 collective-permute-start.2
  690.2 11.9 copy-start.80
  690.2 12.4 copy-start.87
  690.2 12.4 copy-start.97
  690.2 12.4 copy-start.86
  690.2 12.4 copy-start.96
  707.0 51.1 %copy-start.12 = (f32[4,24,96,64]{2,3,1,0:T(8,128)S(1)}, f32[4,24,96,64]{2,3,1,0:T(8,128)}, u32[]{:S(2)}) copy-start(f32[4,24,96,64]{2,3,1,0:T(8,128)} %fusion.60) | copy-start | bytes 7077892
  707.0 51.1 %copy-start.69 = (bf16[64,64]{1,0:T(8,128)(2,1)S(1)}, bf16[64,64]{1,0:T(8,128)(2,1)}, u32[]{:S(2)}) copy-start(bf16[64,64]{1,0:T(8,128)(2,1)} %param.23) | copy-start | bytes 24580
  (68 other events, 253.6 us)
Sparse Core Ops, SparseCore 0:
  660.9 1116.5 all-reduce.11
where the time goes:
time: 1820 us; the launch traced here: 1800 us
  waiting for transfers between devices  1110 us (61%)
  local copies, waits for them, and re-layouts  228 us (13%)
  matrix products  202 us (11%)
  other arithmetic  133 us (7%)
  blocking collectives  85.5 us (5%)
  starting transfers between devices  27.5 us (2%)
    psum x1, waiting for transfers between devices, per_device(): lax.psum((gradients[0], gradients[1], gradients[2], gradients[3], gradien...  1020 us
    all_to_all x1, waiting for transfers between devices, per_device(): lax.all_to_all(qkv_local, 'row', split_axis=3, concat_axis=1, tiled=True)  53.7 us
    psum x1, blocking collectives, per_device(): lax.psum((gradients[0], gradients[1], gradients[2], gradients[3], gradien...  44.1 us
    unnamed x231, local copies, waits for them, and re-layouts  42.4 us
  transfers between devices with their start and end apart: 9, of which 5 were waited for; matrix products, arithmetic and copies ran while one was open for 4% of the time, Pallas kernels for 0%

commit v1 on v0

v1 whole, which is shorter than its diff:
```python
import jax
import jax.numpy as jnp
from jax import lax
from jax.sharding import PartitionSpec as P

GROUPS = 32
HEADS = 12
HEAD_DIM = 64
PATCH = 4
FULL = 96
SMALL = 56
SIDE = FULL // PATCH
TOK = SIDE * SIDE
f32 = jnp.float32
bf16 = jnp.bfloat16


def mm(a, b):
    return lax.dot_general(a, b, (((1,), (0,)), ((), ())), preferred_element_type=f32)


def mm_nt(a, b):
    return lax.dot_general(a, b, (((1,), (1,)), ((), ())), preferred_element_type=f32)


def mm_tn(a, b):
    return lax.dot_general(a, b, (((0,), (0,)), ((), ())), preferred_element_type=f32)


def gelu_both(z):
    cdf = 0.5 * (1.0 + lax.erf(z * 0.7071067811865476))
    pdf = 0.3989422804014327 * jnp.exp(-0.5 * z * z)
    return z * cdf, cdf + z * pdf


def spread4(w):
    return jnp.kron(jnp.eye(PATCH, dtype=w.dtype), w)


def band(taps):
    c, _, d = taps.shape
    zero = jnp.zeros((c, d), taps.dtype)
    mats = []
    for di in range(3):
        rows = []
        for src in (0, 1, 2, 3, -1, 4):
            rows.append(
                [taps[:, 3 * di + src - j + 1] if abs(src - j) <= 1 else zero for j in range(PATCH)]
            )
        mats.append(jnp.block(rows))
    return mats


def fold_band(mats, c, d):
    taps = []
    srcs = (0, 1, 2, 3, -1, 4)
    for di in range(3):
        for dj in range(3):
            total = 0.0
            for j in range(PATCH):
                k = srcs.index(j + dj - 1)
                total = total + mats[di][k * c : (k + 1) * c, j * d : (j + 1) * d]
            taps.append(total)
    return jnp.stack(taps, axis=1)


def fold4(m, c, d):
    return sum(m[j * c : (j + 1) * c, j * d : (j + 1) * d] for j in range(PATCH))


def widen(v):
    c = v.shape[2] // PATCH
    g = v.reshape(PATCH, SIDE, SIDE, PATCH * c)
    up = jnp.pad(g[3:4, :-1], ((0, 0), (1, 0), (0, 0), (0, 0)))
    down = jnp.pad(g[0:1, 1:], ((0, 0), (0, 1), (0, 0), (0, 0)))
    g = jnp.concatenate([up, g, down], axis=0)
    left = jnp.pad(g[:, :, :-1, 3 * c :], ((0, 0), (0, 0), (1, 0), (0, 0)))
    right = jnp.pad(g[:, :, 1:, :c], ((0, 0), (0, 0), (0, 1), (0, 0)))
    g = jnp.concatenate([g, left, right], axis=-1)
    return g.reshape(PATCH + 2, TOK, 6 * c)


def conv3(wide, mats):
    c = wide.shape[2]
    out = 0.0
    for di in range(3):
        out = out + mm(wide[di : di + PATCH].reshape(PATCH * TOK, c), mats[di])
    return out


def group_matrix(chans, lanes):
    lane = jnp.arange(lanes) % chans // (chans // GROUPS)
    return (lane[:, None] == lane[None, :]).astype(f32)


def lane_group_sum(row, gmat):
    return jnp.dot(row, gmat, precision=lax.Precision.HIGHEST)


def gn_stats(v, keep, count, gmat):
    masked = v * keep
    s1 = lane_group_sum(jnp.sum(masked, axis=0, keepdims=True), gmat)
    s2 = lane_group_sum(jnp.sum(masked * v, axis=0, keepdims=True), gmat)
    mean = s1 / count
    rstd = lax.rsqrt(s2 / count - mean * mean + 1e-05)
    return mean, rstd


def gn_back(g, n, rstd, keep, count, gmat, gain):
    c1 = jnp.sum(g, axis=0, keepdims=True)
    c2 = jnp.sum(g * n, axis=0, keepdims=True)
    s1 = lane_group_sum(c1 * gain, gmat) / count
    s2 = lane_group_sum(c2 * gain, gmat) / count
    return rstd * (g * gain - s1 - n * s2) * keep, c2, c1


def ln_stats(h):
    mean = jnp.mean(h, axis=-1, keepdims=True)
    cen = h - mean
    rstd = lax.rsqrt(jnp.mean(cen * cen, axis=-1, keepdims=True) + 1e-05)
    return cen * rstd, rstd


def ln_back(gy, n, rstd, gain):
    gn = gy * gain
    gh = rstd * (
        gn - jnp.mean(gn, axis=-1, keepdims=True) - n * jnp.mean(gn * n, axis=-1, keepdims=True)
    )
    return gh, jnp.sum(gy * n, axis=0), jnp.sum(gy, axis=0)


def per_image(x, side, cot, params):
    (
        conv_in,
        conv_mid,
        conv_out,
        conv_skip,
        norm_gain,
        norm_bias,
        patch_weight,
        patch_bias,
        attn_gain,
        attn_bias,
        qkv_weight,
        out_weight,
        mlp_gain,
        mlp_bias,
        up_weight,
        up_bias,
        down_weight,
        down_bias,
    ) = params
    c0 = conv_in.shape[0]
    c3 = conv_out.shape[1]
    rows = PATCH * TOK
    pos = jnp.arange(TOK)
    limit = side // PATCH
    keep = ((pos // SIDE < limit) & (pos % SIDE < limit)).astype(f32)[:, None]
    keep4 = jnp.tile(keep, (PATCH, 1))
    cells = (side * side).astype(f32)
    x = (x.reshape(rows, PATCH * c0) * keep4.astype(bf16)).astype(bf16)
    g64 = group_matrix(c0, PATCH * c0)
    g256 = group_matrix(c3, PATCH * c3)
    gains = [jnp.tile(v, PATCH)[None] for v in (norm_gain[:c0], norm_gain[c0 : 2 * c0], norm_gain[2 * c0 :])]
    biases = [jnp.tile(v, PATCH)[None] for v in (norm_bias[:c0], norm_bias[c0 : 2 * c0], norm_bias[2 * c0 :])]
    n1count = cells * (c0 // GROUPS)
    n3count = cells * (c3 // GROUPS)
    w_in = spread4(conv_in)
    w_out = spread4(conv_out)
    w_skip = spread4(conv_skip)
    b_fwd = band(conv_mid)
    b_bwd = band(jnp.flip(conv_mid, axis=1).transpose(2, 1, 0))
    v1 = mm(x, w_in)
    m1, r1 = gn_stats(v1, keep4, n1count, g64)
    n1 = (v1 - m1) * r1
    a1, d1 = gelu_both(n1 * gains[0] + biases[0])
    p1 = (a1 * keep4).astype(bf16)
    wide = widen(p1.reshape(PATCH, TOK, PATCH * c0))
    v2 = conv3(wide, b_fwd)
    m2, r2 = gn_stats(v2, keep4, n1count, g64)
    n2 = (v2 - m2) * r2
    a2, d2 = gelu_both(n2 * gains[1] + biases[1])
    p2 = (a2 * keep4).astype(bf16)
    v3 = mm(p2, w_out)
    m3, r3 = gn_stats(v3, keep4, n3count, g256)
    n3 = (v3 - m3) * r3
    z3 = n3 * gains[2] + biases[2] + mm(x, w_skip)
    a3, d3 = gelu_both(z3)
    stem = (a3 * keep4).astype(bf16).reshape(PATCH, TOK, PATCH * c3)
    pw = patch_weight.reshape(PATCH, PATCH * c3, -1)
    hidden = patch_bias
    for i in range(PATCH):
        hidden = hidden + mm(stem[i], pw[i])
    na, ra = ln_stats(hidden)
    normed = (na * attn_gain + attn_bias).astype(bf16)
    qkv = mm(normed, qkv_weight).astype(bf16)
    qkv = qkv.reshape(TOK, 3, HEADS, HEAD_DIM).transpose(1, 2, 0, 3)
    q, k, v = qkv[0], qkv[1], qkv[2]
    scale = HEAD_DIM**-0.5
    scores = jnp.einsum("hqe,hke->hqk", q, k, preferred_element_type=f32) * scale
    scores = jnp.where(keep[:, 0] > 0, scores, -1000000000.0)
    expo = jnp.exp(scores - jnp.max(scores, axis=-1, keepdims=True))
    probs = expo / jnp.sum(expo, axis=-1, keepdims=True)
    probs_low = probs.astype(bf16)
    mixed = jnp.einsum("hqk,hke->hqe", probs_low, v, preferred_element_type=f32).astype(bf16)
    attended = mixed.transpose(1, 0, 2).reshape(TOK, -1)
    hidden2 = hidden + mm(attended, out_weight)
    nm, rm = ln_stats(hidden2)
    normed2 = (nm * mlp_gain + mlp_bias).astype(bf16)
    pre = mm(normed2, up_weight) + up_bias
    act, dact = gelu_both(pre)
    act = act.astype(bf16)
    block_out = ((hidden2 + mm(act, down_weight) + down_bias) * keep).astype(bf16)
    g_final = cot.astype(f32) * keep
    g_low = g_final.astype(bf16)
    grad_down_bias = jnp.sum(g_final, axis=0)
    grad_down = mm_tn(act, g_low)
    g_pre = mm_nt(g_low, down_weight) * dact
    grad_up_bias = jnp.sum(g_pre, axis=0)
    g_pre = g_pre.astype(bf16)
    grad_up = mm_tn(normed2, g_pre)
    g_ln, grad_mlp_gain, grad_mlp_bias = ln_back(mm_nt(g_pre, up_weight), nm, rm, mlp_gain)
    g_h2 = g_final + g_ln
    g_h2_low = g_h2.astype(bf16)
    grad_out = mm_tn(attended, g_h2_low)
    g_att = mm_nt(g_h2_low, out_weight).astype(bf16).reshape(TOK, HEADS, HEAD_DIM).transpose(1, 0, 2)
    g_v = jnp.einsum("hqk,hqe->hke", probs_low, g_att, preferred_element_type=f32)
    g_p = jnp.einsum("hqe,hke->hqk", g_att, v, preferred_element_type=f32)
    g_s = probs * (g_p - jnp.sum(g_p * probs, axis=-1, keepdims=True))
    g_s = g_s.astype(bf16)
    g_q = jnp.einsum("hqk,hke->hqe", g_s, k, preferred_element_type=f32) * scale
    g_k = jnp.einsum("hqk,hqe->hke", g_s, q, preferred_element_type=f32) * scale
    g_qkv = jnp.stack([g_q, g_k, g_v]).astype(bf16).transpose(2, 0, 1, 3).reshape(TOK, -1)
    grad_qkv = mm_tn(normed, g_qkv)
    g_ln, grad_attn_gain, grad_attn_bias = ln_back(mm_nt(g_qkv, qkv_weight), na, ra, attn_gain)
    g_h = g_h2 + g_ln
    grad_patch_bias = jnp.sum(g_h, axis=0)
    g_h = g_h.astype(bf16)
    grad_patch = jnp.concatenate([mm_tn(stem[i], g_h) for i in range(PATCH)], axis=0)
    g_stem = jnp.concatenate([mm_nt(g_h, pw[i]) for i in range(PATCH)], axis=0)
    g_z = g_stem * d3 * keep4
    g_z_low = g_z.astype(bf16)
    grad_skip = fold4(mm_tn(x, g_z_low), c0, c3)
    g_v3, gain3, bias3 = gn_back(g_z, n3, r3, keep4, n3count, g256, gains[2])
    g_v3 = g_v3.astype(bf16)
    grad_cout = fold4(mm_tn(p2, g_v3), c0, c3)
    g_2 = mm_nt(g_v3, w_out) * d2 * keep4
    g_v2, gain2, bias2 = gn_back(g_2, n2, r2, keep4, n1count, g64, gains[1])
    g_v2 = g_v2.astype(bf16)
    grad_mid = fold_band(
        [mm_tn(wide[di : di + PATCH].reshape(rows, 6 * c0), g_v2) for di in range(3)], c0, c0
    )
    g_wide = widen(g_v2.reshape(PATCH, TOK, PATCH * c0))
    g_1 = conv3(g_wide, b_bwd) * d1 * keep4
    g_v1, gain1, bias1 = gn_back(g_1, n1, r1, keep4, n1count, g64, gains[0])
    g_v1 = g_v1.astype(bf16)
    grad_in = fold4(mm_tn(x, g_v1), c0, c0)
    input_grad = (mm_nt(g_v1, w_in) + mm_nt(g_z_low, w_skip)) * keep4

    def lanes(v):
        return jnp.sum(v.reshape(PATCH, -1), axis=0)

    grads = (
        grad_in,
        grad_mid,
        grad_cout,
        grad_skip,
        jnp.concatenate([lanes(gain1), lanes(gain2), lanes(gain3)]),
        jnp.concatenate([lanes(bias1), lanes(bias2), lanes(bias3)]),
        grad_patch,
        grad_patch_bias,
        grad_attn_gain,
        grad_attn_bias,
        grad_qkv,
        grad_out,
        grad_mlp_gain,
        grad_mlp_bias,
        grad_up,
        grad_up_bias,
        grad_down,
        grad_down_bias,
    )
    return block_out, input_grad.reshape(PATCH, TOK, PATCH * c0), grads


def per_device(stem_input, group, *rest):
    params, cot = rest[:-1], rest[-1]
    images, row_count, col_count, c0 = stem_input.shape
    ranks = lax.axis_size("row")
    assert images == ranks
    side = jnp.where(group[lax.axis_index("row")] == 1, FULL, SMALL).astype(jnp.int32)
    strips = row_count // PATCH
    x = stem_input.reshape(images, strips, PATCH, SIDE, PATCH * c0).transpose(0, 2, 1, 3, 4)
    x = lax.all_to_all(x, "row", 0, 0, tiled=True)
    x = x.transpose(1, 0, 2, 3, 4).reshape(PATCH, TOK, PATCH * c0)
    cot_in = lax.all_to_all(cot, "row", 0, 0, tiled=True).reshape(TOK, -1)
    block_out, input_grad, grads = per_image(x, side, cot_in, params)
    block_out = block_out.reshape(images, -1, block_out.shape[-1])
    block_out = lax.all_to_all(block_out, "row", 0, 0, tiled=True)
    ig = input_grad.astype(bf16).reshape(PATCH, ranks, strips, SIDE, PATCH * c0).transpose(1, 0, 2, 3, 4)
    ig = lax.all_to_all(ig, "row", 0, 0, tiled=True)
    ig = ig.transpose(0, 2, 1, 3, 4).reshape(images, row_count, col_count, c0).astype(f32)
    big = [i for i, g in enumerate(grads) if g.size > 100000]
    sums = {}
    for i, s in zip(big, lax.psum([grads[i].astype(bf16) for i in big], ("img", "row"))):
        sums[i] = s
    small = [i for i in range(len(grads)) if i not in big]
    flat = jnp.concatenate([grads[i].reshape(-1) for i in small])
    flat = lax.psum(flat, ("img", "row"))
    at = 0
    for i in small:
        sums[i] = flat[at : at + grads[i].size].reshape(grads[i].shape)
        at += grads[i].size
    rank = lax.axis_index("row")
    shares = []
    for i in range(len(grads)):
        part = grads[i].shape[0] // ranks
        shares.append(lax.dynamic_slice_in_dim(sums[i], rank * part, part, 0).astype(f32))
    return (block_out, ig) + tuple(shares)


def solution(mesh):
    rep = P()
    in_specs = (P("img", "row", None, None), P("img")) + (rep,) * 18 + (P("img", "row", None),)
    dims = (2, 3, 2, 2, 1, 1, 2, 1, 1, 1, 2, 2, 1, 1, 2, 1, 2, 1)
    out_specs = (P("img", "row", None), P("img", "row", None, None)) + tuple(
        P("row", *([None] * (n - 1))) for n in dims
    )
    return jax.shard_map(
        per_device, mesh=mesh, in_specs=in_specs, out_specs=out_specs, check_vma=False
    )
```

time: 1820 us -> 863 us (0.47)
  waiting for transfers between devices: 1110 us -> 421 us
  local copies, waits for them, and re-layouts: 228 us -> 89.2 us
  blocking collectives: 85.5 us -> 0 us
  matrix products: 202 us -> 177 us
    psum x1 -> x2, waiting for transfers between devices: 1020 us -> 391 us  [the longest x1 293 us: per_device(): lax.psum([grads[i].astype(bf16) for i in big], ('img', 'row'))]
    psum x7 -> x0, blocking collectives: 85.5 us -> none  [the longest x1 44.1 us: per_device(): lax.psum((gradients[0], gradients[1], gradients[2], gradients[3], gradien...]
    all_to_all x4, waiting for transfers between devices: 96.7 us -> 30.3 us  [the longest x1 22.9 us: per_device(): ig = lax.all_to_all(ig, 'row', 0, 0, tiled=True)]
    reshape x7 -> x5, local copies, waits for them, and re-layouts: 58.7 us -> 5.32 us  [the longest x1 4.28 us: per_device(): stem_input.reshape(images, strips, PATCH, SIDE, PATCH * c0)]
    all_to_all x6 -> x0, local copies, waits for them, and re-layouts: 39.8 us -> none  [the longest x2 17.7 us: per_device(): lax.all_to_all(qkv_local, 'row', split_axis=3, concat_axis=1, tiled=True)]
    convert_element_type x11 -> x18, other arithmetic: 86.1 us -> 46.5 us  [the longest x5 13.5 us: per_device(): lax.dynamic_slice_in_dim(sums[i], rank * part, part, 0).astype(f32)]
    sub x0 -> x1, other arithmetic: none -> 22.6 us  [per_image(): expo = jnp.exp(scores - jnp.max(scores, axis=-1, keepdims=True))]
    unnamed x6 -> x36, other arithmetic: 2.21 us -> 23.6 us
  transfers between devices with their start and end apart: 9 -> 6, of which waited for: 5 -> 4; matrix products, arithmetic and copies ran while one was open for 4% -> 13% of each run, Pallas kernels for 0% -> 0%
where the time goes in v1:
time: 863 us; the launch traced here: 855 us
  waiting for transfers between devices  421 us (49%)
  matrix products  177 us (21%)
  other arithmetic  133 us (15%)
  local copies, waits for them, and re-layouts  89.2 us (10%)
  between operations  17 us (2%)
  starting transfers between devices  16.8 us (2%)
    psum x1, waiting for transfers between devices, per_device(): lax.psum([grads[i].astype(bf16) for i in big], ('img', 'row'))  293 us
    psum x1, waiting for transfers between devices, per_device(): flat = lax.psum(flat, ('img', 'row'))  97.8 us
    dot_general x14, matrix products, mm_tn(): lax.dot_general(a, b, (((0,), (0,)), ((), ())), preferred_element_type=f32)  44.1 us
    dot_general x17, matrix products, mm(): lax.dot_general(a, b, (((1,), (0,)), ((), ())), preferred_element_type=f32)  43.7 us
    dot_general x11, matrix products, mm_nt(): lax.dot_general(a, b, (((1,), (1,)), ((), ())), preferred_element_type=f32)  31.5 us
    unnamed x267, local copies, waits for them, and re-layouts  26.8 us
    unnamed x36, other arithmetic  23.6 us
    all_to_all x1, waiting for transfers between devices, per_device(): ig = lax.all_to_all(ig, 'row', 0, 0, tiled=True)  22.9 us
  transfers between devices with their start and end apart: 6, of which 4 were waited for; matrix products, arithmetic and copies ran while one was open for 13% of the time, Pallas kernels for 0%

profile of v1, /device:TPU:0, one launch (start us, length us, event | category | flops | bytes accessed | tf_op | source)
XLA Modules:
  0.0 854.6 jit_solution(18336108930348350401)
XLA Ops:
  7.2 4.5 all-to-all-start.2
  53.9 3.9 copy.62
  57.8 4.3 reshape.565
  69.9 4.3 all-to-all-start
  83.4 7.4 all-to-all-done
  109.0 7.8 multiply_convert_fusion.2
  122.7 3.9 convolution_convert_fusion.3
  126.6 4.5 copy.64
  131.1 10.0 %fusion.104 = f32[12,576,576]{1,2,0:T(8,128)} fusion(bf16[3,12,576,64]{2,3,1,0:T(8,128)(2,1)} %bitcast.273), kind=kOutput, calls=%fused_computation.187 | convolution fusion | flops 509607936 | bytes 17891328 | tf_op jit(solution)/shard_map/hqe,hke->hqk/dot_general | solution.py:200
  141.2 22.6 %fusion.232 = (f32[12,576]{1,0:T(8,128)}, f32[12,576,576]{1,2,0:T(8,128)}) fusion(f32[12,576,576]{1,2,0:T(8,128)} %fusion.104, pred[576]{0:T(1024)(128)(4,1)} %broadcast_compare_fusion), kind=kOutput, calls=%fused_computation.518 | output fusion | flops 23888448 | bytes 31878720 | tf_op jit(solution)/shard_map/sub | solution.py:202
  163.8 8.1 fusion.69
  173.4 6.7 multiply_convert_fusion.3
  180.2 6.7 fusion.234
  186.9 3.9 multiply_reduce_fusion.8
  190.7 6.3 convolution_convert_fusion.2
  204.2 10.0 %fusion.92 = bf16[1,12,576,64]{2,3,1,0:T(8,128)(2,1)} fusion(bf16[12,576,64]{1,2,0:T(8,128)(2,1)} %bitcast.295, f32[12,576,576]{1,2,0:T(8,128)} %get-tuple-element.180, f32[12,576]{1,0:T(8,128)} %get-tuple-element.179), kind=kOutput, calls=%fused_computation.169 | convolution fusion | flops 518012928 | bytes 17722368 | tf_op jit(solution)/shard_map/hqk,hqe->hke/dot_general | solution.py:227
  214.2 15.2 %multiply_reduce_fusion = (f32[12,576]{1,0:T(8,128)S(1)}, f32[12,576,576]{1,2,0:T(8,128)}) fusion(f32[12,576,576]{1,2,0:T(8,128)} %get-tuple-element.180, f32[12,576]{1,0:T(8,128)} %get-tuple-element.179, bf16[12,576,64]{1,2,0:T(8,128)(2,1)} %bitcast.296, bf16[3,12,576,64]{2,3,1,0:T(8,128)(2,1)} %bitcast.275), kind=kOutput, calls=%fused_computation.2 | convolution fusion | flops 521544960 | bytes 35654656 | tf_op jit(solution)/shard_map/hqe,hke->hqk/dot_general | solution.py:228
  229.4 12.4 %multiply_convert_fusion = bf16[12,576,576]{1,2,0:T(8,128)(2,1)S(1)} fusion(f32[12,576,576]{1,2,0:T(8,128)} %get-tuple-element.185, f32[12,576]{1,0:T(8,128)S(1)} %get-tuple-element.184, f32[12,576,576]{1,2,0:T(8,128)} %get-tuple-element.180, f32[12,576]{1,0:T(8,128)S(1)} %copy-done.53), kind=kLoop, calls=%fused_computation.1 | loop fusion | flops 15925248 | bytes 39868416 | tf_op jit(solution)/shard_map/convert_element_type | solution.py:230
  241.8 3.9 fusion.91
  245.8 3.0 fusion.90
  250.2 3.7 multiply_reduce_fusion.9
  253.9 5.2 convolution_convert_fusion
  260.4 2.6 convolution_convert_fusion.5
  263.0 2.6 convolution_convert_fusion.6
  265.6 2.6 convolution_convert_fusion.7
  268.2 2.6 convolution_convert_fusion.4
  274.2 2.5 fusion.86
  278.3 13.4 %fusion.212 = (f32[1024]{0:T(1024)S(1)}, f32[1024]{0:T(1024)S(1)}, f32[2304,1024]{1,0:T(8,128)}) fusion(f32[1024]{0:T(1024)S(1)} %copy-done.57, f32[2304,1024]{1,0:T(8,128)S(1)} %bitcast.263, f32[1024]{0:T(1024)S(1)} %copy-done.55, f32[2304]{0:T(1024)S(1)} %copy-done.27, f32[2304,1024]{1,0:T(8,128)S(1)} %bitcast.279, f32[576,1024]{1,0:T(8,128)S(1)} %fusion.75, ...), kind=kLoop, calls=%fused_computation.499 | loop fusion | flops 42465280 | bytes 37774336 | tf_op jit(solution)/shard_map/reduce_sum | solution.py:110
  295.6 8.0 multiply_convert_fusion.1
  306.2 3.8 fusion.214
  324.8 3.7 fusion.213
  330.7 7.8 convolution_convert_fusion.1
  344.5 5.1 fusion.53
  350.2 3.1 multiply_convert_fusion.4
  354.3 11.3 %concatenate.48 = f32[82176]{0:T(1024)} concatenate(f32[4096]{0:T(1024)S(1)} %reshape.577, f32[36864]{0:T(1024)S(1)} %copy-done.37, f32[16384]{0:T(1024)S(1)} %bitcast.306, f32[16384]{0:T(1024)S(1)} %bitcast.307, f32[64]{0:T(128)S(1)} %reduce_sum.337, f32[64]{0:T(128)S(1)} %copy-done.103, f32[256]{0:T(256)S(1)} %copy-done.96, f32[64]{0:T(128)S(1)} %reduce_sum.340, ...), dimensions={0} | concatenate | bytes 657408 | tf_op jit(solution)/shard_map/concatenate | solution.py:308
  365.8 6.8 pad_maximum_fusion
  376.1 7.3 multiply_convert_fusion.10
  383.4 4.4 all-to-all-start.1
  387.8 5.2 fusion.55
  394.8 97.8 %all-reduce.12.cloned.1.call-done = f32[82176]{0:T(1024)} async-done(((f32[82176]{0:T(1024)}), f32[82176]{0:T(1024)}) %all-reduce.12.cloned.1.call-update) | async-done | bytes 328720 | tf_op jit(solution)/shard_map/psum | solution.py:309
  500.0 3.5 all-to-all-start.3
  506.9 22.9 %all-to-all-done.3 = bf16[4,4,6,24,256]{4,3,1,2,0:T(8,128)(2,1)S(1)} async-done(((bf16[4,4,6,24,256]{4,3,1,2,0:T(8,128)(2,1)}), bf16[4,4,6,24,256]{4,3,1,2,0:T(8,128)(2,1)S(1)}, u32[]{:S(2)}, u32[]{:S(2)}) %all-to-all-start.3) | async-done | bytes 1179680 | tf_op jit(solution)/shard_map/all_to_all | solution.py:301
  530.1 2.9 reshape.589
  533.0 5.6 copy.74
  538.6 293.3 %all-reduce.14.cloned.1.call-done = (bf16[4096,768]{1,0:T(8,128)(2,1)}, bf16[768,2304]{1,0:T(8,128)(2,1)}, bf16[768,768]{1,0:T(8,128)(2,1)}, bf16[768,3072]{1,0:T(8,128)(2,1)}, bf16[3072,768]{1,0:T(8,128)(2,1)}) async-done(((bf16[4096,768]{1,0:T(8,128)(2,1)}, bf16[768,2304]{1,0:T(8,128)(2,1)}, bf16[768,768]{1,0:T(8,128)(2,1)}, bf16[768,3072]{1,0:T(8,128)(2,1)}, bf16[3072,768]{1,0:T(8,128)(2,1)}), ...) | async-done | bytes 20447248 | tf_op jit(solution)/shard_map/psum | solution.py:305
  836.2 2.9 dynamic-slice_convert_fusion.2
  839.1 2.8 dynamic-slice_convert_fusion.1
  841.9 3.5 dynamic-slice_convert_fusion
  (467 shorter events, 151.4 us)
Async XLA Ops:
  7.2 115.5 %copy-start = (bf16[768,2304]{1,0:T(8,128)(2,1)S(1)}, bf16[768,2304]{1,0:T(8,128)(2,1)}, u32[]{:S(2)}) copy-start(bf16[768,2304]{1,0:T(8,128)(2,1)} %param.57) | copy-start | bytes 10616836
  7.2 62.7 %all-to-all-start.2 = ((bf16[4,144,768]{2,1,0:T(8,128)(2,1)}), bf16[4,144,768]{2,1,0:T(8,128)(2,1)}, u32[]{:S(2)}, u32[]{:S(2)}) async-start(bf16[4,144,768]{2,1,0:T(8,128)(2,1)} %param.65), calls=%async_computation.2 | async-start | bytes 1769472 | tf_op jit(solution)/shard_map/all_to_all | solution.py:296
  13.6 23.7 %copy-start.90 = (bf16[4,4]{1,0:T(4,128)(2,1)}, bf16[4,4]{1,0:T(4,128)(2,1)S(1)}, u32[]{:S(2)}) copy-start(bf16[4,4]{1,0:T(4,128)(2,1)S(1)} %fusion.208) | copy-start | bytes 100
  18.8 11.5 %copy-start.50 = (f32[576]{0:T(1024)}, f32[576]{0:T(1024)S(1)}, u32[]{:S(2)}) copy-start(f32[576]{0:T(1024)S(1)} %fusion.206) | copy-start | bytes 6916
  31.8 5.6 copy-start.25
  69.9 20.8 %all-to-all-start = ((bf16[4,4,6,24,256]{4,3,1,2,0:T(8,128)(2,1)}), bf16[4,4,6,24,256]{4,3,1,2,0:T(8,128)(2,1)}, u32[]{:S(2)}, u32[]{:S(2)}) async-start(bf16[4,4,6,24,256]{4,3,1,2,0:T(8,128)(2,1)} %bitcast.282), calls=%async_computation | async-start | bytes 2359296 | tf_op jit(solution)/shard_map/all_to_all | solution.py:294
  74.2 418.4 %all-reduce.12.cloned.1.call-start = ((), (), s32[]{:S(2)}) async-start(), calls=%async_computation.4 | async-start | bytes 663552 | tf_op jit(solution)/shard_map/psum | solution.py:309
  83.4 9.0 %copy-start.26 = (f32[2304]{0:T(1024)S(1)}, f32[2304]{0:T(1024)}, u32[]{:S(2)}) copy-start(f32[2304]{0:T(1024)} %copy-done.25) | copy-start | bytes 27652
  106.2 10.6 %copy-start.2 = (f32[2304,1024]{1,0:T(8,128)}, f32[2304,1024]{1,0:T(8,128)S(1)}, u32[]{:S(2)}) copy-start(f32[2304,1024]{1,0:T(8,128)S(1)} %get-tuple-element.174) | copy-start | bytes 28311556
  106.3 10.6 %slice-start.7 = ((s8[6291456]{0:T(1024)(128)(4,1)}), s8[4194304]{0:T(1024)(128)(4,1)S(1)}, s32[]{:S(2)}) async-start(s8[6291456]{0:T(1024)(128)(4,1)} %bitcast.300), calls=%async_computation.13 | async-start | bytes 8388608
  109.0 7.9 copy-start.54
  109.0 7.9 copy-start.56
  109.0 7.9 slice-start.8
  163.8 8.1 copy-start.4
  163.8 8.1 copy-start.30
  171.9 8.2 slice-start.15
  173.0 24.1 %copy-start.8 = (f32[576,768]{1,0:T(8,128)}, f32[576,768]{1,0:T(8,128)S(1)}, u32[]{:S(2)}) copy-start(f32[576,768]{1,0:T(8,128)S(1)} %get-tuple-element.182) | copy-start | bytes 5308420
  173.4 6.7 copy-start.34
  173.4 6.7 slice-start.16
  173.4 13.4 %slice-start.13 = ((s8[4718592]{0:T(1024)(128)(4,1)}), s8[4194304]{0:T(1024)(128)(4,1)S(1)}, s32[]{:S(2)}) async-start(s8[4718592]{0:T(1024)(128)(4,1)} %bitcast.332), calls=%async_computation.19 | async-start | bytes 8388608
  180.2 6.7 slice-start.14
  190.7 6.3 copy-start.51
  214.2 15.2 %copy-start.53 = (f32[12,576]{1,0:T(8,128)S(1)}, f32[12,576]{1,0:T(8,128)}, u32[]{:S(2)}) copy-start(f32[12,576]{1,0:T(8,128)} %get-tuple-element.179) | copy-start | bytes 82948
  250.2 10.2 %slice-start.11 = ((s8[4718592]{0:T(1024)(128)(4,1)}), s8[4194304]{0:T(1024)(128)(4,1)S(1)}, s32[]{:S(2)}) async-start(s8[4718592]{0:T(1024)(128)(4,1)} %bitcast.304), calls=%async_computation.17 | async-start | bytes 8388608
  253.9 5.2 copy-start.19
  253.9 6.5 slice-start.12
  265.6 5.2 slice-start.9
  270.8 6.0 slice-start.3
  278.3 14.6 %copy-start.59 = (f32[1,2,4,128]{3,1,2,0:T(2,128)S(1)}, f32[1,2,4,128]{3,1,2,0:T(2,128)}, u32[]{:S(2)}) copy-start(f32[1,2,4,128]{3,1,2,0:T(2,128)} %copy.81) | copy-start | bytes 12292
  278.3 14.6 %copy-start.100 = (s32[1024]{0:T(1024)S(1)}, s32[1024]{0:T(1024)}, u32[]{:S(2)}) copy-start(s32[1024]{0:T(1024)} %add_select_fusion.4) | copy-start | bytes 12292
  295.6 8.0 copy-start.29
  330.6 7.9 copy-start.68
  330.6 8.4 copy-start.67
  330.6 10.6 %copy-start.78 = (f32[4,64]{1,0:T(4,128)S(1)}, f32[4,64]{1,0:T(4,128)}, u32[]{:S(2)}) copy-start(f32[4,64]{1,0:T(4,128)} %reshape_broadcast_in_dim.22) | copy-start | bytes 3076
  330.6 11.2 %copy-start.80 = (f32[4,64]{1,0:T(4,128)S(1)}, f32[4,64]{1,0:T(4,128)}, u32[]{:S(2)}) copy-start(f32[4,64]{1,0:T(4,128)} %reshape_broadcast_in_dim.19) | copy-start | bytes 3076
  330.7 11.7 %copy-start.24 = (f32[384,256]{1,0:T(8,128)S(1)}, f32[384,256]{1,0:T(8,128)}, u32[]{:S(2)}) copy-start(f32[384,256]{1,0:T(8,128)} %fusion.238) | copy-start | bytes 1179652
  330.7 11.9 %copy-start.23 = (f32[384,256]{1,0:T(8,128)S(1)}, f32[384,256]{1,0:T(8,128)}, u32[]{:S(2)}) copy-start(f32[384,256]{1,0:T(8,128)} %fusion.239) | copy-start | bytes 1179652
  330.7 12.2 %copy-start.22 = (f32[384,256]{1,0:T(8,128)S(1)}, f32[384,256]{1,0:T(8,128)}, u32[]{:S(2)}) copy-start(f32[384,256]{1,0:T(8,128)} %fusion.240) | copy-start | bytes 1179652
  338.5 5.7 copy-start.60
  365.7 6.9 copy-start.20
  365.7 466.2 %all-reduce.14.cloned.1.call-start = ((), (), s32[]{:S(2)}) async-start(), calls=%async_computation.5 | async-start | bytes 40894464 | tf_op jit(solution)/shard_map/psum | solution.py:305
  365.7 6.8 copy-start.32
  383.4 116.6 %all-to-all-start.1 = ((bf16[4,144,768]{2,1,0:T(8,128)(2,1)}), bf16[4,144,768]{2,1,0:T(8,128)(2,1)}, u32[]{:S(2)}, u32[]{:S(2)}) async-start(bf16[4,144,768]{2,1,0:T(8,128)(2,1)} %bitcast.297), calls=%async_computation.1 | async-start | bytes 1769472 | tf_op jit(solution)/shard_map/all_to_all | solution.py:299
  387.8 5.3 copy-start.39
  492.6 10.9 %copy-start.36 = (f32[82176]{0:T(1024)S(1)}, f32[82176]{0:T(1024)}, u32[]{:S(2)}) copy-start(f32[82176]{0:T(1024)} %all-reduce.12.cloned.1.call-done) | copy-start | bytes 986116
  492.6 11.0 %slice-start.6 = ((f32[82176]{0:T(1024)}), f32[36864]{0:T(1024)S(1)}, s32[]{:S(2)}) async-start(f32[82176]{0:T(1024)} %all-reduce.12.cloned.1.call-done), calls=%async_computation.12 | async-start | bytes 294912 | tf_op jit(solution)/shard_map/slice | solution.py:312
  500.0 29.8 %all-to-all-start.3 = ((bf16[4,4,6,24,256]{4,3,1,2,0:T(8,128)(2,1)}), bf16[4,4,6,24,256]{4,3,1,2,0:T(8,128)(2,1)S(1)}, u32[]{:S(2)}, u32[]{:S(2)}) async-start(bf16[4,4,6,24,256]{4,3,1,2,0:T(8,128)(2,1)} %bitcast.258), calls=%async_computation.3 | async-start | bytes 2359296 | tf_op jit(solution)/shard_map/all_to_all | solution.py:301
  841.9 5.6 copy-start.1
  (86 other events, 177.5 us)
Sparse Core Ops, SparseCore 0:
  365.8 126.7 all-reduce.11
  500.7 331.0 all-reduce.13

commit v2 on v1

--- a/solution.py
+++ b/solution.py
@@ -1,6 +1,8 @@
 import jax
 import jax.numpy as jnp
 from jax import lax
+from jax.experimental import pallas as pl
+from jax.experimental.pallas import tpu as pltpu
 from jax.sharding import PartitionSpec as P
 
 GROUPS = 32
@@ -129,7 +131,73 @@
     return gh, jnp.sum(gy * n, axis=0), jnp.sum(gy, axis=0)
 
 
-def per_image(x, side, cot, params):
+def attend_kernel(keep_ref, q_ref, k_ref, v_ref, o_ref, l_ref):
+    scale = HEAD_DIM**-0.5
+    valid = keep_ref[...] > 0
+    outs = []
+    for h in range(2):
+        lanes = slice(h * HEAD_DIM, (h + 1) * HEAD_DIM)
+        q, k, v = q_ref[:, lanes], k_ref[:, lanes], v_ref[:, lanes]
+        s = jnp.where(valid, mm_nt(k, q) * scale, -1000000000.0)
+        top = jnp.max(s, axis=0, keepdims=True)
+        e = jnp.exp(s - top)
+        total = jnp.sum(e, axis=0, keepdims=True)
+        outs.append(mm_tn(v, e.astype(bf16)) / total)
+        l_ref[0, h : h + 1, :] = top + jnp.log(total)
+    o_ref[...] = jnp.concatenate(outs, axis=0).T.astype(bf16)
+
+def attend(qkv, keep):
+    tok, width3 = qkv.shape
+    pairs = HEADS // 2
+    two = 2 * HEAD_DIM
+    def spec(kind):
+        return pl.BlockSpec((tok, two), lambda h: (0, kind * pairs + h))
+    return pl.pallas_call(
+        attend_kernel, grid=(pairs,),
+        in_specs=[pl.BlockSpec((tok, 1), lambda h: (0, 0)), spec(0), spec(1), spec(2)],
+        out_specs=[spec(0), pl.BlockSpec((1, 2, tok), lambda h: (h, 0, 0))],
+        out_shape=[jax.ShapeDtypeStruct((tok, width3 // 3), bf16), jax.ShapeDtypeStruct((pairs, 2, tok), f32)],
+        compiler_params=pltpu.CompilerParams(vmem_limit_bytes=40*1024*1024),
+        name="attend",
+    )(keep, qkv, qkv, qkv)
+
+def attend_back_kernel(keep_ref, q_ref, k_ref, v_ref, g_ref, l_ref, gq_ref, gk_ref, gv_ref):
+    scale = HEAD_DIM**-0.5
+    valid = keep_ref[...] > 0
+    gqs, gks, gvs = [], [], []
+    for h in range(2):
+        lanes = slice(h * HEAD_DIM, (h + 1) * HEAD_DIM)
+        q, k, v, g = q_ref[:, lanes], k_ref[:, lanes], v_ref[:, lanes], g_ref[:, lanes]
+        s = jnp.where(valid, mm_nt(k, q) * scale, -1000000000.0)
+        p = jnp.exp(s - l_ref[0, h : h + 1, :])
+        gp = mm_nt(v, g)
+        dot = jnp.sum(gp * p, axis=0, keepdims=True)
+        gs = (p * (gp - dot)).astype(bf16)
+        gvs.append(mm(p.astype(bf16), g))
+        gks.append(mm(gs, q) * scale)
+        gqs.append(mm_tn(k, gs) * scale)
+    gq_ref[...] = jnp.concatenate(gqs, axis=0).T.astype(bf16)
+    gk_ref[...] = jnp.concatenate(gks, axis=1).astype(bf16)
+    gv_ref[...] = jnp.concatenate(gvs, axis=1).astype(bf16)
+
+def attend_back(qkv, keep, g, logs):
+    tok, width3 = qkv.shape
+    pairs = HEADS // 2
+    two = 2 * HEAD_DIM
+    def spec(kind):
+        return pl.BlockSpec((tok, two), lambda h: (0, kind * pairs + h))
+    o = jax.ShapeDtypeStruct((tok, width3 // 3), bf16)
+    return pl.pallas_call(
+        attend_back_kernel, grid=(pairs,),
+        in_specs=[pl.BlockSpec((tok, 1), lambda h: (0, 0)), spec(0), spec(1), spec(2), spec(0), pl.BlockSpec((1, 2, tok), lambda h: (h, 0, 0))],
+        out_specs=[spec(0)] * 3,
+        out_shape=[o, o, o],
+        compiler_params=pltpu.CompilerParams(vmem_limit_bytes=40*1024*1024),
+        name="attend_back",
+    )(keep, qkv, qkv, qkv, g, logs)
+
+
+def per_image(x, side, cot, params, flows):
     (
         conv_in,
         conv_mid,
@@ -194,16 +262,7 @@
     na, ra = ln_stats(hidden)
     normed = (na * attn_gain + attn_bias).astype(bf16)
     qkv = mm(normed, qkv_weight).astype(bf16)
-    qkv = qkv.reshape(TOK, 3, HEADS, HEAD_DIM).transpose(1, 2, 0, 3)
-    q, k, v = qkv[0], qkv[1], qkv[2]
-    scale = HEAD_DIM**-0.5
-    scores = jnp.einsum("hqe,hke->hqk", q, k, preferred_element_type=f32) * scale
-    scores = jnp.where(keep[:, 0] > 0, scores, -1000000000.0)
-    expo = jnp.exp(scores - jnp.max(scores, axis=-1, keepdims=True))
-    probs = expo / jnp.sum(expo, axis=-1, keepdims=True)
-    probs_low = probs.astype(bf16)
-    mixed = jnp.einsum("hqk,hke->hqe", probs_low, v, preferred_element_type=f32).astype(bf16)
-    attended = mixed.transpose(1, 0, 2).reshape(TOK, -1)
+    attended, logs = attend(qkv, keep)
     hidden2 = hidden + mm(attended, out_weight)
     nm, rm = ln_stats(hidden2)
     normed2 = (nm * mlp_gain + mlp_bias).astype(bf16)
@@ -214,46 +273,49 @@
     g_final = cot.astype(f32) * keep
     g_low = g_final.astype(bf16)
     grad_down_bias = jnp.sum(g_final, axis=0)
-    grad_down = mm_tn(act, g_low)
+    g_low = flows.begin("down", mm_tn(act, g_low), g_low)
     g_pre = mm_nt(g_low, down_weight) * dact
     grad_up_bias = jnp.sum(g_pre, axis=0)
     g_pre = g_pre.astype(bf16)
-    grad_up = mm_tn(normed2, g_pre)
+    g_pre = flows.begin("up", mm_tn(normed2, g_pre), g_pre)
+    g_pre = flows.pump(g_pre, "up")
     g_ln, grad_mlp_gain, grad_mlp_bias = ln_back(mm_nt(g_pre, up_weight), nm, rm, mlp_gain)
     g_h2 = g_final + g_ln
     g_h2_low = g_h2.astype(bf16)
     grad_out = mm_tn(attended, g_h2_low)
-    g_att = mm_nt(g_h2_low, out_weight).astype(bf16).reshape(TOK, HEADS, HEAD_DIM).transpose(1, 0, 2)
-    g_v = jnp.einsum("hqk,hqe->hke", probs_low, g_att, preferred_element_type=f32)
-    g_p = jnp.einsum("hqe,hke->hqk", g_att, v, preferred_element_type=f32)
-    g_s = probs * (g_p - jnp.sum(g_p * probs, axis=-1, keepdims=True))
-    g_s = g_s.astype(bf16)
-    g_q = jnp.einsum("hqk,hke->hqe", g_s, k, preferred_element_type=f32) * scale
-    g_k = jnp.einsum("hqk,hqe->hke", g_s, q, preferred_element_type=f32) * scale
-    g_qkv = jnp.stack([g_q, g_k, g_v]).astype(bf16).transpose(2, 0, 1, 3).reshape(TOK, -1)
+    g_att = mm_nt(g_h2_low, out_weight).astype(bf16)
+    g_att = flows.pump(g_att, "att")
+    g_qkv = jnp.concatenate(attend_back(qkv, keep, g_att, logs), axis=1)
+    g_qkv = flows.pump(g_qkv, "qkv")
     grad_qkv = mm_tn(normed, g_qkv)
+    g_qkv = flows.begin("qkv", jnp.concatenate([grad_qkv, grad_out], axis=1), g_qkv)
+    g_qkv = flows.pump(g_qkv, "ln")
     g_ln, grad_attn_gain, grad_attn_bias = ln_back(mm_nt(g_qkv, qkv_weight), na, ra, attn_gain)
     g_h = g_h2 + g_ln
     grad_patch_bias = jnp.sum(g_h, axis=0)
     g_h = g_h.astype(bf16)
     grad_patch = jnp.concatenate([mm_tn(stem[i], g_h) for i in range(PATCH)], axis=0)
+    g_h = flows.begin("patch", grad_patch, g_h)
+    g_h = flows.pump(g_h, "patch")
     g_stem = jnp.concatenate([mm_nt(g_h, pw[i]) for i in range(PATCH)], axis=0)
+    g_stem = flows.pump(g_stem, "stem")
     g_z = g_stem * d3 * keep4
     g_z_low = g_z.astype(bf16)
     grad_skip = fold4(mm_tn(x, g_z_low), c0, c3)
+    g_z = flows.pump(g_z, "z")
     g_v3, gain3, bias3 = gn_back(g_z, n3, r3, keep4, n3count, g256, gains[2])
-    g_v3 = g_v3.astype(bf16)
+    g_v3 = flows.pump(g_v3.astype(bf16), "v3")
     grad_cout = fold4(mm_tn(p2, g_v3), c0, c3)
     g_2 = mm_nt(g_v3, w_out) * d2 * keep4
     g_v2, gain2, bias2 = gn_back(g_2, n2, r2, keep4, n1count, g64, gains[1])
-    g_v2 = g_v2.astype(bf16)
+    g_v2 = flows.pump(g_v2.astype(bf16), "v2")
     grad_mid = fold_band(
         [mm_tn(wide[di : di + PATCH].reshape(rows, 6 * c0), g_v2) for di in range(3)], c0, c0
     )
     g_wide = widen(g_v2.reshape(PATCH, TOK, PATCH * c0))
     g_1 = conv3(g_wide, b_bwd) * d1 * keep4
     g_v1, gain1, bias1 = gn_back(g_1, n1, r1, keep4, n1count, g64, gains[0])
-    g_v1 = g_v1.astype(bf16)
+    g_v1 = flows.pump(g_v1.astype(bf16), "v1")
     grad_in = fold4(mm_tn(x, g_v1), c0, c0)
     input_grad = (mm_nt(g_v1, w_in) + mm_nt(g_z_low, w_skip)) * keep4
 
@@ -267,20 +329,165 @@
         grad_skip,
         jnp.concatenate([lanes(gain1), lanes(gain2), lanes(gain3)]),
         jnp.concatenate([lanes(bias1), lanes(bias2), lanes(bias3)]),
-        grad_patch,
+        None,
         grad_patch_bias,
         grad_attn_gain,
         grad_attn_bias,
-        grad_qkv,
-        grad_out,
+        None,
+        None,
         grad_mlp_gain,
         grad_mlp_bias,
-        grad_up,
+        None,
         grad_up_bias,
-        grad_down,
+        None,
         grad_down_bias,
     )
     return block_out, input_grad.reshape(PATCH, TOK, PATCH * c0), grads
+
+
+def swap(v, axis, step):
+    count = lax.axis_size(axis)
+    return lax.ppermute(v, axis, [(i, i ^ step) for i in range(count)])
+
+
+def plus(a, b):
+    return (a.astype(f32) + b.astype(f32)).astype(a.dtype)
+
+
+def steps_of(axis):
+    count = lax.axis_size(axis)
+    return [1 << b for b in range(count.bit_length() - 1)]
+
+
+def tie(x, *others):
+    return lax.optimization_barrier((x,) + others)
+
+
+def flow(whole, order):
+    ranks = lax.axis_size("row")
+    rank = lax.axis_index("row")
+    me = lax.axis_index("img")
+    rows = whole.shape[0] // ranks
+    cut = whole.reshape(ranks, rows, *whole.shape[1:])
+    rels = [int(bin(ranks + r)[:2:-1], 2) for r in range(ranks)]
+    v = jnp.stack([lax.dynamic_index_in_dim(cut, rank ^ r, 0, keepdims=False) for r in rels])
+    undo = []
+    for axis, step in order:
+        if axis == "row":
+            n = v.shape[0] // 2
+            keep, send = v[:n], v[n:]
+        else:
+            n = v.shape[1] // 2
+            odd = (me & step) > 0
+            low, high = v[:, :n], v[:, n:]
+            send = jnp.where(odd, low, high)
+            keep = jnp.where(odd, high, low)
+            undo.append(step)
+        got = yield send, axis, step
+        v = plus(keep, got)
+    for step in reversed(undo):
+        odd = (me & step) > 0
+        got = yield v, "img", step
+        v = jnp.concatenate([jnp.where(odd, got, v), jnp.where(odd, v, got)], axis=1)
+    yield v[0].astype(f32), None, None
+
+
+XY = (("row", 1), ("row", 2), ("img", 1), ("img", 2), ("img", 4))
+
+
+class Flows:
+    def __init__(self, plan):
+        self.plan = plan
+        self.live = {}
+        self.out = {}
+
+    def send(self, name, item, x):
+        what, axis, step = item
+        if axis is None:
+            self.out[name] = what
+            return x
+        x, what = tie(x, what)
+        self.live[name][1] = swap(what, axis, step)
+        return x
+
+    def begin(self, name, whole, x):
+        order = [(a, s) for a in ("row", "img") for s in steps_of(a)]
+        gen = flow(whole.astype(bf16), order)
+        self.live[name] = [gen, None]
+        return self.send(name, next(gen), x)
+
+    def advance(self, name, x):
+        gen, got = self.live[name]
+        x, got = tie(x, got)
+        return self.send(name, gen.send(got), x)
+
+    def pump(self, x, point):
+        for name in self.plan.get(point, ()):
+            x = self.advance(name, x)
+        return x
+
+    def finish(self):
+        busy = True
+        while busy:
+            busy = False
+            for name in list(self.live):
+                if name not in self.out:
+                    gen, got = self.live[name]
+                    what, axis, step = gen.send(got)
+                    if axis is None:
+                        self.out[name] = what
+                    else:
+                        self.live[name][1] = swap(what, axis, step)
+                        busy = True
+        return self.out
+
+
+PLAN = {
+    "up": ("down",),
+    "att": ("up",),
+    "qkv": ("down",),
+    "ln": ("up",),
+    "patch": ("qkv",),
+    "stem": ("down", "patch"),
+    "z": ("down", "up"),
+    "v3": ("down", "up", "qkv"),
+    "v2": ("down", "up", "qkv"),
+    "v1": ("down", "up", "qkv"),
+}
+
+
+def img_sum_small(v):
+    for step in steps_of("img"):
+        v = v + swap(v, "img", step)
+    return v
+
+
+def row_scatter(pieces):
+    pieces = list(pieces)
+    for step in steps_of("row"):
+        for r in range(0, len(pieces), step):
+            if r & step:
+                pieces[r ^ step] = pieces[r ^ step] + swap(pieces[r], "row", step)
+    return pieces[0]
+
+
+def small_sums(grads, ranks):
+    rank = lax.axis_index("row")
+    some = [g for g in grads if g is not None]
+    flat = jnp.concatenate([g.reshape(ranks, -1) for g in some], axis=1)
+    flat = jnp.pad(flat, ((0, 0), (0, -flat.shape[1] % 1024))).reshape(ranks, -1, 128)
+    pieces = [lax.dynamic_index_in_dim(flat, rank ^ r, 0, keepdims=False) for r in range(ranks)]
+    flat = img_sum_small(row_scatter(pieces)).reshape(-1)
+    at = 0
+    sums = []
+    for g in grads:
+        if g is None:
+            sums.append(None)
+            continue
+        n = g.size // ranks
+        sums.append(flat[at : at + n].reshape((g.shape[0] // ranks,) + g.shape[1:]))
+        at += n
+    return sums
 
 
 def per_device(stem_input, group, *rest):
@@ -294,28 +501,19 @@
     x = lax.all_to_all(x, "row", 0, 0, tiled=True)
     x = x.transpose(1, 0, 2, 3, 4).reshape(PATCH, TOK, PATCH * c0)
     cot_in = lax.all_to_all(cot, "row", 0, 0, tiled=True).reshape(TOK, -1)
-    block_out, input_grad, grads = per_image(x, side, cot_in, params)
+    flows = Flows(PLAN)
+    block_out, input_grad, grads = per_image(x, side, cot_in, params, flows)
     block_out = block_out.reshape(images, -1, block_out.shape[-1])
     block_out = lax.all_to_all(block_out, "row", 0, 0, tiled=True)
     ig = input_grad.astype(bf16).reshape(PATCH, ranks, strips, SIDE, PATCH * c0).transpose(1, 0, 2, 3, 4)
     ig = lax.all_to_all(ig, "row", 0, 0, tiled=True)
     ig = ig.transpose(0, 2, 1, 3, 4).reshape(images, row_count, col_count, c0).astype(f32)
-    big = [i for i, g in enumerate(grads) if g.size > 100000]
-    sums = {}
-    for i, s in zip(big, lax.psum([grads[i].astype(bf16) for i in big], ("img", "row"))):
-        sums[i] = s
-    small = [i for i in range(len(grads)) if i not in big]
-    flat = jnp.concatenate([grads[i].reshape(-1) for i in small])
-    flat = lax.psum(flat, ("img", "row"))
-    at = 0
-    for i in small:
-        sums[i] = flat[at : at + grads[i].size].reshape(grads[i].shape)
-        at += grads[i].size
-    rank = lax.axis_index("row")
-    shares = []
-    for i in range(len(grads)):
-        part = grads[i].shape[0] // ranks
-        shares.append(lax.dynamic_slice_in_dim(sums[i], rank * part, part, 0).astype(f32))
+    shares = small_sums(grads, ranks)
+    big = flows.finish()
+    width = big["qkv"].shape[1] * 3 // 4
+    shares[6] = big["patch"]
+    shares[10], shares[11] = big["qkv"][:, :width], big["qkv"][:, width:]
+    shares[14], shares[16] = big["up"], big["down"]
     return (block_out, ig) + tuple(shares)
 
 

time: 863 us -> 558 us (0.65)
  waiting for transfers between devices: 421 us -> 87.1 us
  matrix products: 177 us -> 127 us
  starting transfers between devices: 16.8 us -> 55.9 us
  Pallas kernels: 0 us -> 25.4 us
  other arithmetic: 133 us -> 158 us
  between operations: 17 us -> 4.58 us
    psum x2 -> x0, waiting for transfers between devices: 391 us -> none  [the longest x1 293 us: per_device(): lax.psum([grads[i].astype(bf16) for i in big], ('img', 'row'))]
    ppermute x0 -> x38, waiting for transfers between devices: none -> 79.3 us  [swap(): return lax.ppermute(v, axis, [(i, i ^ step) for i in range(count)])]
    dot_general x6 -> x0, matrix products: 50.2 us -> none  [the longest x1 15.2 us: per_image(): g_p = jnp.einsum('hqe,hke->hqk', g_att, v, preferred_element_type=f32)]
    ppermute x0 -> x38, starting transfers between devices: none -> 38.9 us  [swap(): return lax.ppermute(v, axis, [(i, i ^ step) for i in range(count)])]
    pallas_call x0 -> x2, Pallas kernels: none -> 25.4 us  [the longest x1 15.3 us: attend_back(): pl.pallas_call(attend_back_kernel, grid=(pairs,), in_specs=[pl.BlockSpec(...]
    all_to_all x1, waiting for transfers between devices: 22.9 us -> 0.01 us  [per_device(): ig = lax.all_to_all(ig, 'row', 0, 0, tiled=True)]
    sub x1 -> x0, other arithmetic: 22.6 us -> none  [per_image(): expo = jnp.exp(scores - jnp.max(scores, axis=-1, keepdims=True))]
    select_n x0 -> x24, other arithmetic: none -> 18.2 us  [the longest x12 10.8 us: flow(): jnp.where(odd, got, v)]
  transfers between devices with their start and end apart: 6 -> 42, of which waited for: 4 -> 13; matrix products, arithmetic and copies ran while one was open for 13% -> 57% of each run, Pallas kernels for 0% -> 3%
where the time goes in v2:
time: 558 us; the launch traced here: 550 us
  other arithmetic  158 us (28%)
  matrix products  127 us (23%)
  local copies, waits for them, and re-layouts  91.6 us (16%)
  waiting for transfers between devices  87.1 us (16%)
  starting transfers between devices  55.9 us (10%)
  Pallas kernels  25.4 us (5%)
    ppermute x38, waiting for transfers between devices, swap(): return lax.ppermute(v, axis, [(i, i ^ step) for i in range(count)])  79.3 us
    dot_general x11, matrix products, mm_nt(): lax.dot_general(a, b, (((1,), (1,)), ((), ())), preferred_element_type=f32)  44.7 us
    ppermute x38, starting transfers between devices, swap(): return lax.ppermute(v, axis, [(i, i ^ step) for i in range(count)])  38.9 us
    dot_general x17, matrix products, mm(): lax.dot_general(a, b, (((1,), (0,)), ((), ())), preferred_element_type=f32)  37.6 us
    dot_general x14, matrix products, mm_tn(): lax.dot_general(a, b, (((0,), (0,)), ((), ())), preferred_element_type=f32)  36.5 us
    unnamed x373, local copies, waits for them, and re-layouts  29.6 us
    convert_element_type x20, other arithmetic, plus(): return (a.astype(f32) + b.astype(f32)).astype(a.dtype)  28.3 us
    unnamed x33, other arithmetic  22.6 us
  transfers between devices with their start and end apart: 42, of which 13 were waited for; matrix products, arithmetic and copies ran while one was open for 57% of the time, Pallas kernels for 3%

profile of v2, /device:TPU:0, one launch (start us, length us, event | category | flops | bytes accessed | tf_op | source)
XLA Modules:
  0.0 549.8 jit_solution(4837812831617469655)
XLA Ops:
  0.7 4.5 all-to-all-start.2
  48.1 3.9 copy.50
  52.1 4.3 reshape.632
  64.3 4.5 all-to-all-start
  77.4 7.9 %all-to-all-done = bf16[4,4,6,24,256]{4,3,1,2,0:T(8,128)(2,1)} async-done(((bf16[4,4,6,24,256]{4,3,1,2,0:T(8,128)(2,1)}), bf16[4,4,6,24,256]{4,3,1,2,0:T(8,128)(2,1)}, u32[]{:S(2)}, u32[]{:S(2)}) %all-to-all-start) | async-done | bytes 1179680 | tf_op jit(solution)/shard_map/all_to_all | solution.py:501
  103.1 7.6 %multiply_convert_fusion.1 = (bf16[2304,1024]{1,0:T(8,128)(2,1)S(1)}, f32[2304,1024]{1,0:T(8,128)}) fusion(f32[2304]{0:T(1024)S(1)} %copy-done.83, bf16[2304,256]{1,0:T(8,128)(2,1)S(1)} %bitcast.292, bf16[256,1024]{1,0:T(8,128)(2,1)S(1)} %bitcast.282, f32[1024]{0:T(1024)S(1)} %bitcast.309, f32[1024]{0:T(1024)S(1)} %bitcast.304, ...), kind=kOutput, calls=%fused_computation.14 | convolution fusion | flops 1233911808 | bytes 25322496 | tf_op jit(solution)/shard_map/dot_general | solution.py:21
  120.5 10.1 %attend.1 = (bf16[576,768]{1,0:T(8,128)(2,1)S(1)}, f32[6,2,576]{2,1,0:T(2,128)S(1)}) custom-call(f32[576,1]{1,0:T(8,128)S(1)} %copy-done.4, bf16[576,2304]{1,0:T(8,128)(2,1)S(1)} %convolution_convert_fusion.3.q_ref.k_ref.v_ref, bf16[576,2304]{1,0:T(8,128)(2,1)S(1)} %convolution_convert_fusion.3.q_ref.k_ref.v_ref, ...), custom_call_target="tpu_custom_call" | custom-call | tf_op jit(solution)/shard_map/attend/pallas_call | solution.py:155
  132.1 6.5 %multiply_convert_fusion.2 = (bf16[576,3072]{1,0:T(8,128)(2,1)S(1)}, f32[576,3072]{1,0:T(8,128)}) fusion(f32[3072]{0:T(1024)S(1)} %copy-done.157, bf16[768,3072]{1,0:T(8,128)(2,1)S(1)} %bitcast.331, f32[576,768]{1,0:T(8,128)S(1)} %get-tuple-element.388, f32[768]{0:T(1024)S(1)} %copy-done.160, f32[768]{0:T(1024)S(1)} %copy-done.142, ...), kind=kOutput, calls=%fused_computation.37 | convolution fusion | flops 2730737664 | bytes 17127936 | tf_op jit(solution)/shard_map/dot_general | solution.py:21
  138.7 3.9 multiply_convert_fusion.7
  142.6 4.2 all-to-all-start.1
  146.8 6.1 %convolution_convert_fusion.2 = bf16[3072,768]{1,0:T(8,128)(2,1)S(1)} fusion(bf16[576,3072]{1,0:T(8,128)(2,1)} %copy-done.165, bf16[576,768]{1,0:T(8,128)(2,1)} %fusion.56), kind=kOutput, calls=%fused_computation.47 | convolution fusion | flops 2720268288 | bytes 9142272 | tf_op jit(solution)/shard_map/dot_general | solution.py:29
  156.7 10.6 %fusion.207 = (f32[3072]{0:T(1024)}, bf16[576,3072]{1,0:T(8,128)(2,1)}) fusion(f32[576,3072]{1,0:T(8,128)} %get-tuple-element.390, f32[3072]{0:T(1024)S(1)} %copy-done.158, bf16[576,768]{1,0:T(8,128)(2,1)S(1)} %copy-done.89, bf16[3072,768]{1,0:T(8,128)(2,1)} %param.63), kind=kOutput, calls=%fused_computation.586 | convolution fusion | flops 2739139584 | bytes 16244736 | tf_op jit(solution)/shard_map/dot_general | solution.py:25
  168.7 6.7 %convolution_convert_fusion.1 = bf16[768,3072]{1,0:T(8,128)(2,1)S(1)} fusion(bf16[576,3072]{1,0:T(8,128)(2,1)} %get-tuple-element.112, f32[576,768]{1,0:T(8,128)} %copy-done.16, f32[768]{0:T(1024)} %param.60, f32[768]{0:T(1024)} %param.59, f32[576]{0:T(1024)} %copy-done.122, f32[576]{0:T(1024)S(1)} %broadcast_multiply_fusion.8), kind=kOutput, calls=%fused_computation.46 | convolution fusion | flops 2722480128 | bytes 10037760 | tf_op jit(solution)/shard_map/dot_general | solution.py:29
  180.4 3.1 add_convert_fusion.3
  186.0 7.3 %multiply_reduce_fusion.7 = (f32[768]{0:T(1024)}, f32[576]{0:T(1024)}, f32[576]{0:T(1024)}, f32[768]{0:T(1024)}, f32[576,768]{1,0:T(8,128)}) fusion(f32[576,768]{1,0:T(8,128)S(1)} %copy-done.17, f32[576]{0:T(1024)S(1)} %copy-done.123, f32[576]{0:T(1024)S(1)} %broadcast_multiply_fusion.8, f32[768]{0:T(1024)S(1)} %copy-done.143, ...), kind=kOutput, calls=%fused_computation.127 | convolution fusion | flops 2721887744 | bytes 11814912 | tf_op jit(solution)/shard_map/dot_general | solution.py:25
  199.4 3.0 multiply_add_fusion.3
  204.0 2.7 add_convert_fusion.2
  207.7 15.3 %attend_back.1 = (bf16[576,768]{1,0:T(8,128)(2,1)S(1)}, bf16[576,768]{1,0:T(8,128)(2,1)S(1)}, bf16[576,768]{1,0:T(8,128)(2,1)S(1)}) custom-call(f32[576,1]{1,0:T(8,128)S(1)} %copy-done.5, bf16[576,2304]{1,0:T(8,128)(2,1)S(1)} %copy-done.3, bf16[576,2304]{1,0:T(8,128)(2,1)S(1)} %copy-done.3, bf16[576,2304]{1,0:T(8,128)(2,1)S(1)} %copy-done.3, ...), custom_call_target="tpu_custom_call" | custom-call | tf_op jit(solution)/shard_map/attend_back/pallas_call | solution.py:190
  230.4 3.5 convolution_convert_fusion
  237.3 12.5 %collective-permute-done.3 = bf16[1,192,3072]{2,1,0:T(8,128)(2,1)S(1)} collective-permute-done((bf16[1,192,3072]{2,1,0:T(8,128)(2,1)S(1)}, bf16[1,192,3072]{2,1,0:T(8,128)(2,1)S(1)}, u32[]{:S(2)}, u32[]{:S(2)}) %collective-permute-start.3) | collective-permute-done | bytes 1179680 | tf_op jit(solution)/shard_map/ppermute | solution.py:350
  252.1 3.1 multiply_reduce_fusion.8
  260.3 2.9 convolution_convert_fusion.4
  263.2 3.1 convolution_convert_fusion.5
  274.4 2.9 add_convert_fusion.1
  287.8 2.6 fusion.69
  290.3 3.8 pad_maximum_fusion
  298.0 2.9 add_convert_fusion
  302.3 6.9 %fusion.6 = f32[2304,1024]{1,0:T(8,128)} fusion(f32[2304,1024]{1,0:T(8,128)S(1)} %pad_maximum_fusion, f32[2304,1024]{1,0:T(8,128)S(1)} %bitcast.274, f32[2304]{0:T(1024)S(1)} %copy-done.84), kind=kLoop, calls=%fused_computation.10 | loop fusion | flops 23592960 | bytes 28320768 | tf_op jit(solution)/shard_map/mul | solution.py:302
  312.8 8.1 %fusion.203 = (f32[1024]{0:T(1024)S(1)}, f32[1024]{0:T(1024)S(1)}) fusion(f32[2304,1024]{1,0:T(8,128)} %fusion.6, f32[1024]{0:T(1024)S(1)} %copy-done.116, f32[2304,1024]{1,0:T(8,128)} %copy-done.10, f32[1024]{0:T(1024)S(1)} %copy-done.114), kind=kLoop, calls=%fused_computation.582 | loop fusion | flops 11794432 | bytes 18890752 | tf_op jit(solution)/shard_map/reduce_sum | solution.py:112
  320.9 6.5 %fusion.46 = f32[2304,256]{1,0:T(8,128)} fusion(bf16[256,1024]{1,0:T(8,128)(2,1)S(1)} %bitcast.283, f32[2304,1024]{1,0:T(8,128)} %fusion.6), kind=kOutput, calls=%fused_computation.98 | convolution fusion | flops 1210318848 | bytes 12320768 | tf_op jit(solution)/shard_map/dot_general | solution.py:25
  335.6 5.1 fusion.44
  341.7 8.1 %multiply_convert_fusion = bf16[2304,1024]{1,0:T(8,128)(2,1)S(1)} fusion(f32[2304,1024]{1,0:T(8,128)} %fusion.6, f32[2304,1024]{1,0:T(8,128)} %copy-done.10, f32[1024]{0:T(1024)} %broadcast_divide_fusion, f32[1024]{0:T(1024)} %broadcast_divide_fusion.1, f32[1024]{0:T(1024)S(1)} %bitcast.306, f32[1024]{0:T(1024)} %copy-done.115, f32[1024]{0:T(1024)} %copy-done.113, ...), kind=kLoop, calls=%fused_computation.12 | loop fusion | flops 21233664 | bytes 23622656 | tf_op jit(solution)/shard_map/convert_element_type | solution.py:307
  353.6 2.6 collective-permute-start.13
  360.6 4.6 fusion.205
  394.4 3.3 fusion.204
  423.8 3.9 all-to-all-start.3
  428.2 2.6 collective-permute-start.31
  434.8 3.7 collective-permute-done.31
  438.7 6.8 %collective-permute-done.20 = f32[168,128]{1,0:T(8,128)S(1)} collective-permute-done((f32[168,128]{1,0:T(8,128)S(1)}, f32[168,128]{1,0:T(8,128)S(1)}, u32[]{:S(2)}, u32[]{:S(2)}) %collective-permute-start.20) | collective-permute-done | bytes 86048 | tf_op jit(solution)/shard_map/ppermute | solution.py:350
  458.3 2.6 collective-permute-start.23
  469.2 10.4 %collective-permute-done.25 = bf16[1,512,768]{2,1,0:T(8,128)(2,1)} collective-permute-done((bf16[1,512,768]{2,1,0:T(8,128)(2,1)}, bf16[1,512,768]{2,1,0:T(8,128)(2,1)}, u32[]{:S(2)}, u32[]{:S(2)}) %collective-permute-start.25) | collective-permute-done | bytes 786464 | tf_op jit(solution)/shard_map/ppermute | solution.py:350
  482.8 8.5 %collective-permute-done.26 = bf16[1,256,768]{2,1,0:T(8,128)(2,1)S(1)} collective-permute-done((bf16[1,256,768]{2,1,0:T(8,128)(2,1)S(1)}, bf16[1,256,768]{2,1,0:T(8,128)(2,1)S(1)}, u32[]{:S(2)}, u32[]{:S(2)}) %collective-permute-start.26) | collective-permute-done | bytes 393248 | tf_op jit(solution)/shard_map/ppermute | solution.py:350
  491.5 2.7 collective-permute-start.27
  495.0 6.7 %collective-permute-done.27 = bf16[1,128,768]{2,1,0:T(8,128)(2,1)S(1)} collective-permute-done((bf16[1,128,768]{2,1,0:T(8,128)(2,1)S(1)}, bf16[1,128,768]{2,1,0:T(8,128)(2,1)S(1)}, u32[]{:S(2)}, u32[]{:S(2)}) %collective-permute-start.27) | collective-permute-done | bytes 196640 | tf_op jit(solution)/shard_map/ppermute | solution.py:350
  503.2 9.5 %collective-permute-done.28 = bf16[1,128,768]{2,1,0:T(8,128)(2,1)S(1)} collective-permute-done((bf16[1,128,768]{2,1,0:T(8,128)(2,1)S(1)}, bf16[1,128,768]{2,1,0:T(8,128)(2,1)S(1)}, u32[]{:S(2)}, u32[]{:S(2)}) %collective-permute-start.28) | collective-permute-done | bytes 196640 | tf_op jit(solution)/shard_map/ppermute | solution.py:350
  515.6 2.9 reshape.667
  518.5 5.5 %copy.56 = f32[4,24,96,64]{2,3,1,0:T(8,128)} copy(f32[4,24,96,64]{3,2,1,0:T(8,128)} %reshape.667) | data formatting | bytes 4718592
  530.0 14.9 %collective-permute-done.30 = bf16[1,512,768]{2,1,0:T(8,128)(2,1)S(1)} collective-permute-done((bf16[1,512,768]{2,1,0:T(8,128)(2,1)S(1)}, bf16[1,512,768]{2,1,0:T(8,128)(2,1)S(1)}, u32[]{:S(2)}, u32[]{:S(2)}) %collective-permute-start.30) | collective-permute-done | bytes 786464 | tf_op jit(solution)/shard_map/ppermute | solution.py:350
  (706 shorter events, 270.2 us)
Async XLA Ops:
  0.7 117.4 %copy-start = (bf16[768,2304]{1,0:T(8,128)(2,1)S(1)}, bf16[768,2304]{1,0:T(8,128)(2,1)}, u32[]{:S(2)}) copy-start(bf16[768,2304]{1,0:T(8,128)(2,1)} %param.57) | copy-start | bytes 10616836
  0.7 63.6 %all-to-all-start.2 = ((bf16[4,144,768]{2,1,0:T(8,128)(2,1)}), bf16[4,144,768]{2,1,0:T(8,128)(2,1)}, u32[]{:S(2)}, u32[]{:S(2)}) async-start(bf16[4,144,768]{2,1,0:T(8,128)(2,1)} %param.65), calls=%async_computation.2 | async-start | bytes 1769472 | tf_op jit(solution)/shard_map/all_to_all | solution.py:503
  7.1 23.2 %copy-start.146 = (bf16[4,4]{1,0:T(4,128)(2,1)}, bf16[4,4]{1,0:T(4,128)(2,1)S(1)}, u32[]{:S(2)}) copy-start(bf16[4,4]{1,0:T(4,128)(2,1)S(1)} %fusion.201) | copy-start | bytes 100
  64.3 21.0 %all-to-all-start = ((bf16[4,4,6,24,256]{4,3,1,2,0:T(8,128)(2,1)}), bf16[4,4,6,24,256]{4,3,1,2,0:T(8,128)(2,1)}, u32[]{:S(2)}, u32[]{:S(2)}) async-start(bf16[4,4,6,24,256]{4,3,1,2,0:T(8,128)(2,1)} %bitcast.279), calls=%async_computation | async-start | bytes 2359296 | tf_op jit(solution)/shard_map/all_to_all | solution.py:501
  142.6 37.8 %all-to-all-start.1 = ((bf16[4,144,768]{2,1,0:T(8,128)(2,1)}), bf16[4,144,768]{2,1,0:T(8,128)(2,1)}, u32[]{:S(2)}, u32[]{:S(2)}) async-start(bf16[4,144,768]{2,1,0:T(8,128)(2,1)} %bitcast.293), calls=%async_computation.1 | async-start | bytes 1769472 | tf_op jit(solution)/shard_map/all_to_all | solution.py:507
  156.3 24.1 %collective-permute-start = (bf16[2,768,768]{2,1,0:T(8,128)(2,1)}, bf16[2,768,768]{2,1,0:T(8,128)(2,1)}, u32[]{:S(2)}, u32[]{:S(2)}) collective-permute-start(bf16[2,768,768]{2,1,0:T(8,128)(2,1)} %pad_maximum_fusion.4), channel_id=1, source_target_pairs={{0,1},{1,0},{2,3},{3,2},{4,5},{5,4},{6,7},{7,6},{8,9},{9,8},{10,11... | collective-permute-start | bytes 7077896 | tf_op jit(solution)/shard_map/ppermute | solution.py:350
  178.9 24.5 %collective-permute-start.1 = (bf16[2,192,3072]{2,1,0:T(8,128)(2,1)}, bf16[2,192,3072]{2,1,0:T(8,128)(2,1)}, u32[]{:S(2)}, u32[]{:S(2)}) collective-permute-start(bf16[2,192,3072]{2,1,0:T(8,128)(2,1)} %pad_maximum_fusion.5), channel_id=1, source_target_pairs={{0,1},{1,0},{2,3},{3,2},{4,5},{5,4},{6,7},{7,6},{8,9},{9,8},{10,11... | collective-permute-start | bytes 7077896 | tf_op jit(solution)/shard_map/ppermute | solution.py:350
  196.0 29.0 %collective-permute-start.2 = (bf16[1,768,768]{2,1,0:T(8,128)(2,1)}, bf16[1,768,768]{2,1,0:T(8,128)(2,1)S(1)}, u32[]{:S(2)}, u32[]{:S(2)}) collective-permute-start(bf16[1,768,768]{2,1,0:T(8,128)(2,1)} %slice.678), channel_id=1, source_target_pairs={{0,2},{1,3},{2,0},{3,1},{4,6},{5,7},{6,4},{7,5},{8,10},{9,11},{10,... | collective-permute-start | bytes 3538952 | tf_op jit(solution)/shard_map/ppermute | solution.py:350
  206.8 43.0 %collective-permute-start.3 = (bf16[1,192,3072]{2,1,0:T(8,128)(2,1)S(1)}, bf16[1,192,3072]{2,1,0:T(8,128)(2,1)S(1)}, u32[]{:S(2)}, u32[]{:S(2)}) collective-permute-start(bf16[1,192,3072]{2,1,0:T(8,128)(2,1)S(1)} %slice.679), channel_id=1, source_target_pairs={{0,2},{1,3},{2,0},{3,1},{4,6},{5,7},{6,4},{7,5},{8,10},{9,11},{10,... | collective-permute-start | bytes 3538952 | tf_op jit(solution)/shard_map/ppermute | solution.py:350
  228.1 66.1 %collective-permute-start.5 = (bf16[1,384,768]{2,1,0:T(8,128)(2,1)}, bf16[1,384,768]{2,1,0:T(8,128)(2,1)}, u32[]{:S(2)}, u32[]{:S(2)}) collective-permute-start(bf16[1,384,768]{2,1,0:T(8,128)(2,1)} %broadcast_select_fusion.11), channel_id=1, source_target_pairs={{0,4},{4,0},{8,12},{12,8},{16,20},{20,16},{24,28},{28,24},{1,5},{5... | collective-permute-start | bytes 1769480 | tf_op jit(solution)/shard_map/ppermute | solution.py:350
  255.2 18.7 %collective-permute-start.4 = (bf16[2,192,3072]{2,1,0:T(8,128)(2,1)}, bf16[2,192,3072]{2,1,0:T(8,128)(2,1)}, u32[]{:S(2)}, u32[]{:S(2)}) collective-permute-start(bf16[2,192,3072]{2,1,0:T(8,128)(2,1)} %pad_maximum_fusion.6), channel_id=1, source_target_pairs={{0,1},{1,0},{2,3},{3,2},{4,5},{5,4},{6,7},{7,6},{8,9},{9,8},{10,11... | collective-permute-start | bytes 7077896 | tf_op jit(solution)/shard_map/ppermute | solution.py:350
  258.0 52.2 %collective-permute-start.8 = (bf16[1,96,3072]{2,1,0:T(8,128)(2,1)}, bf16[1,96,3072]{2,1,0:T(8,128)(2,1)}, u32[]{:S(2)}, u32[]{:S(2)}) collective-permute-start(bf16[1,96,3072]{2,1,0:T(8,128)(2,1)} %broadcast_select_fusion.8), channel_id=1, source_target_pairs={{0,4},{4,0},{8,12},{12,8},{16,20},{20,16},{24,28},{28,24},{1,5},{5... | collective-permute-start | bytes 1769480 | tf_op jit(solution)/shard_map/ppermute | solution.py:350
  273.7 24.3 %collective-permute-start.6 = (bf16[2,1024,768]{2,1,0:T(8,128)(2,1)}, bf16[2,1024,768]{2,1,0:T(8,128)(2,1)}, u32[]{:S(2)}, u32[]{:S(2)}) collective-permute-start(bf16[2,1024,768]{2,1,0:T(8,128)(2,1)} %pad_maximum_fusion.2), channel_id=1, source_target_pairs={{0,1},{1,0},{2,3},{3,2},{4,5},{5,4},{6,7},{7,6},{8,9},{9,8},{10,11... | collective-permute-start | bytes 9437192 | tf_op jit(solution)/shard_map/ppermute | solution.py:350
  278.5 77.7 %collective-permute-start.11 = (bf16[1,192,3072]{2,1,0:T(8,128)(2,1)}, bf16[1,192,3072]{2,1,0:T(8,128)(2,1)}, u32[]{:S(2)}, u32[]{:S(2)}) collective-permute-start(bf16[1,192,3072]{2,1,0:T(8,128)(2,1)} %slice.686), channel_id=1, source_target_pairs={{0,2},{1,3},{2,0},{3,1},{4,6},{5,7},{6,4},{7,5},{8,10},{9,11},{10,... | collective-permute-start | bytes 3538952 | tf_op jit(solution)/shard_map/ppermute | solution.py:350
  296.3 13.0 %collective-permute-start.7 = (bf16[1,192,768]{2,1,0:T(8,128)(2,1)S(1)}, bf16[1,192,768]{2,1,0:T(8,128)(2,1)S(1)}, u32[]{:S(2)}, u32[]{:S(2)}) collective-permute-start(bf16[1,192,768]{2,1,0:T(8,128)(2,1)S(1)} %broadcast_select_fusion.23), channel_id=1, source_target_pairs={{0,8},{4,12},{8,0},{12,4},{16,24},{20,28},{24,16},{28,20},{1,9},{5... | collective-permute-start | bytes 884744 | tf_op jit(solution)/shard_map/ppermute | solution.py:350
  327.5 22.3 %collective-permute-start.9 = (bf16[1,96,768]{2,1,0:T(8,128)(2,1)}, bf16[1,96,768]{2,1,0:T(8,128)(2,1)}, u32[]{:S(2)}, u32[]{:S(2)}) collective-permute-start(bf16[1,96,768]{2,1,0:T(8,128)(2,1)} %broadcast_select_fusion.35), channel_id=1, source_target_pairs={{0,16},{4,20},{8,24},{12,28},{16,0},{20,4},{24,8},{28,12},{1,17},{... | collective-permute-start | bytes 442376 | tf_op jit(solution)/shard_map/ppermute | solution.py:350
  335.1 16.7 %collective-permute-start.10 = (bf16[1,48,3072]{2,1,0:T(8,128)(2,1)}, bf16[1,48,3072]{2,1,0:T(8,128)(2,1)}, u32[]{:S(2)}, u32[]{:S(2)}) collective-permute-start(bf16[1,48,3072]{2,1,0:T(8,128)(2,1)} %broadcast_select_fusion.20), channel_id=1, source_target_pairs={{0,8},{4,12},{8,0},{12,4},{16,24},{20,28},{24,16},{28,20},{1,9},{5... | collective-permute-start | bytes 884744 | tf_op jit(solution)/shard_map/ppermute | solution.py:350
  341.3 112.6 %collective-permute-start.24 = (bf16[1,1024,768]{2,1,0:T(8,128)(2,1)}, bf16[1,1024,768]{2,1,0:T(8,128)(2,1)}, u32[]{:S(2)}, u32[]{:S(2)}) collective-permute-start(bf16[1,1024,768]{2,1,0:T(8,128)(2,1)} %slice.689), channel_id=1, source_target_pairs={{0,2},{1,3},{2,0},{3,1},{4,6},{5,7},{6,4},{7,5},{8,10},{9,11},{10,... | collective-permute-start | bytes 4718600 | tf_op jit(solution)/shard_map/ppermute | solution.py:350
  351.4 21.4 %collective-permute-start.12 = (bf16[1,96,768]{2,1,0:T(8,128)(2,1)}, bf16[1,96,768]{2,1,0:T(8,128)(2,1)}, u32[]{:S(2)}, u32[]{:S(2)}) collective-permute-start(bf16[1,96,768]{2,1,0:T(8,128)(2,1)} %add_convert_fusion.21), channel_id=1, source_target_pairs={{0,16},{4,20},{8,24},{12,28},{16,0},{20,4},{24,8},{28,12},{1,17},{... | collective-permute-start | bytes 442376 | tf_op jit(solution)/shard_map/ppermute | solution.py:350
  353.6 25.2 %collective-permute-start.13 = (bf16[1,24,3072]{2,1,0:T(8,128)(2,1)}, bf16[1,24,3072]{2,1,0:T(8,128)(2,1)}, u32[]{:S(2)}, u32[]{:S(2)}) collective-permute-start(bf16[1,24,3072]{2,1,0:T(8,128)(2,1)} %broadcast_select_fusion.32), channel_id=1, source_target_pairs={{0,16},{4,20},{8,24},{12,28},{16,0},{20,4},{24,8},{28,12},{1,17},{... | collective-permute-start | bytes 442376 | tf_op jit(solution)/shard_map/ppermute | solution.py:350
  365.9 15.1 %collective-permute-start.14 = (bf16[1,96,3072]{2,1,0:T(8,128)(2,1)}, bf16[1,96,3072]{2,1,0:T(8,128)(2,1)}, u32[]{:S(2)}, u32[]{:S(2)}) collective-permute-start(bf16[1,96,3072]{2,1,0:T(8,128)(2,1)} %broadcast_select_fusion.7), channel_id=1, source_target_pairs={{0,4},{4,0},{8,12},{12,8},{16,20},{20,16},{24,28},{28,24},{1,5},{5... | collective-permute-start | bytes 1769480 | tf_op jit(solution)/shard_map/ppermute | solution.py:350
  377.2 26.3 %collective-permute-start.15 = (bf16[1,192,768]{2,1,0:T(8,128)(2,1)}, bf16[1,192,768]{2,1,0:T(8,128)(2,1)}, u32[]{:S(2)}, u32[]{:S(2)}) collective-permute-start(bf16[1,192,768]{2,1,0:T(8,128)(2,1)} %pad_maximum_fusion.14), channel_id=1, source_target_pairs={{0,8},{4,12},{8,0},{12,4},{16,24},{20,28},{24,16},{28,20},{1,9},{5... | collective-permute-start | bytes 884744 | tf_op jit(solution)/shard_map/ppermute | solution.py:350
  380.6 30.0 %collective-permute-start.16 = (bf16[1,24,3072]{2,1,0:T(8,128)(2,1)}, bf16[1,24,3072]{2,1,0:T(8,128)(2,1)}, u32[]{:S(2)}, u32[]{:S(2)}) collective-permute-start(bf16[1,24,3072]{2,1,0:T(8,128)(2,1)} %add_convert_fusion.20), channel_id=1, source_target_pairs={{0,16},{4,20},{8,24},{12,28},{16,0},{20,4},{24,8},{28,12},{1,17},{... | collective-permute-start | bytes 442376 | tf_op jit(solution)/shard_map/ppermute | solution.py:350
  387.4 27.6 %collective-permute-start.17 = (bf16[1,48,3072]{2,1,0:T(8,128)(2,1)}, bf16[1,48,3072]{2,1,0:T(8,128)(2,1)}, u32[]{:S(2)}, u32[]{:S(2)}) collective-permute-start(bf16[1,48,3072]{2,1,0:T(8,128)(2,1)} %broadcast_select_fusion.19), channel_id=1, source_target_pairs={{0,8},{4,12},{8,0},{12,4},{16,24},{20,28},{24,16},{28,20},{1,9},{5... | collective-permute-start | bytes 884744 | tf_op jit(solution)/shard_map/ppermute | solution.py:350
  412.4 18.7 %collective-permute-start.35 = (bf16[1,48,3072]{2,1,0:T(8,128)(2,1)}, bf16[1,48,3072]{2,1,0:T(8,128)(2,1)}, u32[]{:S(2)}, u32[]{:S(2)}) collective-permute-start(bf16[1,48,3072]{2,1,0:T(8,128)(2,1)} %pad_maximum_fusion.15), channel_id=1, source_target_pairs={{0,8},{4,12},{8,0},{12,4},{16,24},{20,28},{24,16},{28,20},{1,9},{5... | collective-permute-start | bytes 884744 | tf_op jit(solution)/shard_map/ppermute | solution.py:350
  413.6 43.2 %collective-permute-start.37 = (bf16[1,384,768]{2,1,0:T(8,128)(2,1)}, bf16[1,384,768]{2,1,0:T(8,128)(2,1)}, u32[]{:S(2)}, u32[]{:S(2)}) collective-permute-start(bf16[1,384,768]{2,1,0:T(8,128)(2,1)} %pad_maximum_fusion.10), channel_id=1, source_target_pairs={{0,4},{4,0},{8,12},{12,8},{16,20},{20,16},{24,28},{28,24},{1,5},{5... | collective-permute-start | bytes 1769480 | tf_op jit(solution)/shard_map/ppermute | solution.py:350
  423.8 91.5 %all-to-all-start.3 = ((bf16[4,4,6,24,256]{4,3,1,2,0:T(8,128)(2,1)}), bf16[4,4,6,24,256]{4,3,1,2,0:T(8,128)(2,1)S(1)}, u32[]{:S(2)}, u32[]{:S(2)}) async-start(bf16[4,4,6,24,256]{4,3,1,2,0:T(8,128)(2,1)} %bitcast.258), calls=%async_computation.3 | async-start | bytes 2359296 | tf_op jit(solution)/shard_map/all_to_all | solution.py:509
  428.2 10.3 %collective-permute-start.31 = (bf16[1,24,3072]{2,1,0:T(8,128)(2,1)S(1)}, bf16[1,24,3072]{2,1,0:T(8,128)(2,1)S(1)}, u32[]{:S(2)}, u32[]{:S(2)}) collective-permute-start(bf16[1,24,3072]{2,1,0:T(8,128)(2,1)S(1)} %copy-done.107), channel_id=1, source_target_pairs={{0,16},{4,20},{8,24},{12,28},{16,0},{20,4},{24,8},{28,12},{1,17},{... | collective-permute-start | bytes 442376 | tf_op jit(solution)/shard_map/ppermute | solution.py:350
  430.8 7.8 %collective-permute-start.18 = (f32[168,128]{1,0:T(8,128)S(1)}, f32[168,128]{1,0:T(8,128)S(1)}, u32[]{:S(2)}, u32[]{:S(2)}) collective-permute-start(f32[168,128]{1,0:T(8,128)S(1)} %get-tuple-element.307), channel_id=1, source_target_pairs={{0,1},{1,0},{2,3},{3,2},{4,5},{5,4},{6,7},{7,6},{8,9},{9,8},{10,11... | collective-permute-start | bytes 258056 | tf_op jit(solution)/shard_map/ppermute | solution.py:350
  431.1 22.8 %copy-start.25 = (bf16[2,1024,768]{2,1,0:T(8,128)(2,1)S(1)}, bf16[2,1024,768]{2,1,0:T(8,128)(2,1)}, u32[]{:S(2)}) copy-start(bf16[2,1024,768]{2,1,0:T(8,128)(2,1)} %copy-done.24) | copy-start | bytes 9437188
  431.1 1.6 collective-permute-start.19
  432.6 21.2 %copy-start.47 = (bf16[1,48,3072]{2,1,0:T(8,128)(2,1)}, bf16[1,48,3072]{2,1,0:T(8,128)(2,1)S(1)}, u32[]{:S(2)}) copy-start(bf16[1,48,3072]{2,1,0:T(8,128)(2,1)S(1)} %get-tuple-element.299) | copy-start | bytes 884740
  432.7 21.2 %copy-start.49 = (bf16[1,48,3072]{2,1,0:T(8,128)(2,1)}, bf16[1,48,3072]{2,1,0:T(8,128)(2,1)S(1)}, u32[]{:S(2)}) copy-start(bf16[1,48,3072]{2,1,0:T(8,128)(2,1)S(1)} %get-tuple-element.300) | copy-start | bytes 884740
  432.7 12.7 %collective-permute-start.20 = (f32[168,128]{1,0:T(8,128)S(1)}, f32[168,128]{1,0:T(8,128)S(1)}, u32[]{:S(2)}, u32[]{:S(2)}) collective-permute-start(f32[168,128]{1,0:T(8,128)S(1)} %bitcast_add_fusion), channel_id=1, source_target_pairs={{0,2},{1,3},{2,0},{3,1},{4,6},{5,7},{6,4},{7,5},{8,10},{9,11},{10,... | collective-permute-start | bytes 258056 | tf_op jit(solution)/shard_map/ppermute | solution.py:350
  438.6 12.7 %collective-permute-start.32 = (bf16[1,24,3072]{2,1,0:T(8,128)(2,1)S(1)}, bf16[1,24,3072]{2,1,0:T(8,128)(2,1)S(1)}, u32[]{:S(2)}, u32[]{:S(2)}) collective-permute-start(bf16[1,24,3072]{2,1,0:T(8,128)(2,1)S(1)} %add_convert_fusion.19), channel_id=1, source_target_pairs={{0,16},{4,20},{8,24},{12,28},{16,0},{20,4},{24,8},{28,12},{1,17},{... | collective-permute-start | bytes 442376 | tf_op jit(solution)/shard_map/ppermute | solution.py:350
  445.4 5.5 collective-permute-start.21
  446.9 55.0 %collective-permute-start.36 = (bf16[1,96,3072]{2,1,0:T(8,128)(2,1)}, bf16[1,96,3072]{2,1,0:T(8,128)(2,1)}, u32[]{:S(2)}, u32[]{:S(2)}) collective-permute-start(bf16[1,96,3072]{2,1,0:T(8,128)(2,1)} %pad_maximum_fusion.12), channel_id=1, source_target_pairs={{0,4},{4,0},{8,12},{12,8},{16,20},{20,16},{24,28},{28,24},{1,5},{5... | collective-permute-start | bytes 1769480 | tf_op jit(solution)/shard_map/ppermute | solution.py:350
  450.9 7.3 %collective-permute-start.22 = (f32[168,128]{1,0:T(8,128)S(1)}, f32[168,128]{1,0:T(8,128)S(1)}, u32[]{:S(2)}, u32[]{:S(2)}) collective-permute-start(f32[168,128]{1,0:T(8,128)S(1)} %add.636), channel_id=1, source_target_pairs={{0,8},{4,12},{8,0},{12,4},{16,24},{20,28},{24,16},{28,20},{1,9},{5... | collective-permute-start | bytes 258056 | tf_op jit(solution)/shard_map/ppermute | solution.py:350
  452.1 29.6 %collective-permute-start.33 = (bf16[1,48,3072]{2,1,0:T(8,128)(2,1)}, bf16[1,48,3072]{2,1,0:T(8,128)(2,1)}, u32[]{:S(2)}, u32[]{:S(2)}) collective-permute-start(bf16[1,48,3072]{2,1,0:T(8,128)(2,1)} %pad_maximum_fusion.16), channel_id=1, source_target_pairs={{0,8},{4,12},{8,0},{12,4},{16,24},{20,28},{24,16},{28,20},{1,9},{5... | collective-permute-start | bytes 884744 | tf_op jit(solution)/shard_map/ppermute | solution.py:350
  456.8 22.8 %collective-permute-start.25 = (bf16[1,512,768]{2,1,0:T(8,128)(2,1)}, bf16[1,512,768]{2,1,0:T(8,128)(2,1)}, u32[]{:S(2)}, u32[]{:S(2)}) collective-permute-start(bf16[1,512,768]{2,1,0:T(8,128)(2,1)} %broadcast_select_fusion.2), channel_id=1, source_target_pairs={{0,4},{4,0},{8,12},{12,8},{16,20},{20,16},{24,28},{28,24},{1,5},{5... | collective-permute-start | bytes 2359304 | tf_op jit(solution)/shard_map/ppermute | solution.py:350
  458.3 6.4 %collective-permute-start.23 = (f32[168,128]{1,0:T(8,128)S(1)}, f32[168,128]{1,0:T(8,128)S(1)}, u32[]{:S(2)}, u32[]{:S(2)}) collective-permute-start(f32[168,128]{1,0:T(8,128)S(1)} %add.637), channel_id=1, source_target_pairs={{0,16},{4,20},{8,24},{12,28},{16,0},{20,4},{24,8},{28,12},{1,17},{... | collective-permute-start | bytes 258056 | tf_op jit(solution)/shard_map/ppermute | solution.py:350
  481.0 10.3 %collective-permute-start.26 = (bf16[1,256,768]{2,1,0:T(8,128)(2,1)S(1)}, bf16[1,256,768]{2,1,0:T(8,128)(2,1)S(1)}, u32[]{:S(2)}, u32[]{:S(2)}) collective-permute-start(bf16[1,256,768]{2,1,0:T(8,128)(2,1)S(1)} %broadcast_select_fusion.14), channel_id=1, source_target_pairs={{0,8},{4,12},{8,0},{12,4},{16,24},{20,28},{24,16},{28,20},{1,9},{5... | collective-permute-start | bytes 1179656 | tf_op jit(solution)/shard_map/ppermute | solution.py:350
  482.8 20.4 %copy-start.55 = (bf16[1,48,3072]{2,1,0:T(8,128)(2,1)}, bf16[1,48,3072]{2,1,0:T(8,128)(2,1)S(1)}, u32[]{:S(2)}) copy-start(bf16[1,48,3072]{2,1,0:T(8,128)(2,1)S(1)} %get-tuple-element.301) | copy-start | bytes 884740
  491.5 10.2 %collective-permute-start.27 = (bf16[1,128,768]{2,1,0:T(8,128)(2,1)S(1)}, bf16[1,128,768]{2,1,0:T(8,128)(2,1)S(1)}, u32[]{:S(2)}, u32[]{:S(2)}) collective-permute-start(bf16[1,128,768]{2,1,0:T(8,128)(2,1)S(1)} %broadcast_select_fusion.26), channel_id=1, source_target_pairs={{0,16},{4,20},{8,24},{12,28},{16,0},{20,4},{24,8},{28,12},{1,17},{... | collective-permute-start | bytes 589832 | tf_op jit(solution)/shard_map/ppermute | solution.py:350
  495.0 31.3 %collective-permute-start.34 = (bf16[1,96,3072]{2,1,0:T(8,128)(2,1)}, bf16[1,96,3072]{2,1,0:T(8,128)(2,1)}, u32[]{:S(2)}, u32[]{:S(2)}) collective-permute-start(bf16[1,96,3072]{2,1,0:T(8,128)(2,1)} %pad_maximum_fusion.11), channel_id=1, source_target_pairs={{0,4},{4,0},{8,12},{12,8},{16,20},{20,16},{24,28},{28,24},{1,5},{5... | collective-permute-start | bytes 1769480 | tf_op jit(solution)/shard_map/ppermute | solution.py:350
  501.8 10.9 %collective-permute-start.28 = (bf16[1,128,768]{2,1,0:T(8,128)(2,1)S(1)}, bf16[1,128,768]{2,1,0:T(8,128)(2,1)S(1)}, u32[]{:S(2)}, u32[]{:S(2)}) collective-permute-start(bf16[1,128,768]{2,1,0:T(8,128)(2,1)S(1)} %add_convert_fusion.18), channel_id=1, source_target_pairs={{0,16},{4,20},{8,24},{12,28},{16,0},{20,4},{24,8},{28,12},{1,17},{... | collective-permute-start | bytes 589832 | tf_op jit(solution)/shard_map/ppermute | solution.py:350
  513.6 11.4 %collective-permute-start.29 = (bf16[1,256,768]{2,1,0:T(8,128)(2,1)}, bf16[1,256,768]{2,1,0:T(8,128)(2,1)}, u32[]{:S(2)}, u32[]{:S(2)}) collective-permute-start(bf16[1,256,768]{2,1,0:T(8,128)(2,1)} %pad_maximum_fusion.13), channel_id=1, source_target_pairs={{0,8},{4,12},{8,0},{12,4},{16,24},{20,28},{24,16},{28,20},{1,9},{5... | collective-permute-start | bytes 1179656 | tf_op jit(solution)/shard_map/ppermute | solution.py:350
  526.2 18.7 %collective-permute-start.30 = (bf16[1,512,768]{2,1,0:T(8,128)(2,1)S(1)}, bf16[1,512,768]{2,1,0:T(8,128)(2,1)S(1)}, u32[]{:S(2)}, u32[]{:S(2)}) collective-permute-start(bf16[1,512,768]{2,1,0:T(8,128)(2,1)S(1)} %pad_maximum_fusion.9), channel_id=1, source_target_pairs={{0,4},{4,0},{8,12},{12,8},{16,20},{20,16},{24,28},{28,24},{1,5},{5... | collective-permute-start | bytes 2359304 | tf_op jit(solution)/shard_map/ppermute | solution.py:350
  (174 other events, 848.6 us)
